TPU v7x, 256 devices: a whole 4x4x8 slice. The times are simulated.
256 devices in a mesh: shard: 64 (over z, y, core), rep: 4 (over x).
Axes of the slice: x: 4, y: 4, z: 8, core: 2. Of those that a mesh axis runs over, the one named last changes fastest.
Arguments:
- table: bfloat16 [2048, 1024], P('shard'), may hold values from -6 to 6
- self_feat: bfloat16 [2048, 1024], P(('shard', 'rep')), may hold values from -24 to 24
- weight: bfloat16 [2048, 1024], replicated, may hold values from -0.125 to 0.125
- owners: int32 [2048, 67, 1], P(('shard', 'rep')), may hold values from 0 to 63; in each aligned block of 536 rows (0 to 535, 536 to 1071, ..., all dimensions but the last counted through in order) at most 17 rows name the same one
- item_rows: int32 [2048, 67], P(('shard', 'rep')), may hold values from 0 to 31
- importance: int32 [2048, 50], P(('shard', 'rep')), may hold values from 1 to 32
Outputs:
- grad_self: float32 [2048, 1024], P(('shard', 'rep'))
- grad_weight: float32 [2048, 1024], P(('shard', 'rep'))
- grad_table: float32 [2048, 1024], P(('shard', 'rep'))
Inputs may be any that keep to these rules, and one draw needn't show every extreme that they name: `owners`: among the 536 requests of the queries of one device, no owner is named more than 17 times, and in some device's queries one owner is named exactly 17 times.
All inputs are finite; a program needn't handle non-finite values.
Results may differ from a plain program's by a relative error of at most 0.0095.
Values may be sent and summed in bfloat16 or wider, within the bound.
A program may use at most 64 MiB of HBM per device.

v0:
```python
import jax
import jax.numpy as jnp
from jax import lax
from jax.sharding import PartitionSpec as P

K = 50


MARGIN = 0.5
eps = 1e-06


def forward_backward(fetched, self_feat, weight, importance):
    neighbours = fetched[:, :K].astype(jnp.float32)
    weights_f = importance.astype(jnp.float32)
    shares = weights_f / jnp.sum(weights_f, axis=1, keepdims=True)
    pooled = jnp.einsum("qk,qkf->qf", shares, neighbours).astype(jnp.bfloat16)
    joined = jnp.concatenate([self_feat, pooled], axis=1)
    preact = jnp.dot(joined, weight, preferred_element_type=jnp.float32)
    gate_value = jax.nn.sigmoid(preact)
    activation = preact * gate_value
    act_norm = jnp.sqrt(jnp.sum(activation * activation, axis=1, keepdims=True) + eps)
    unit_vec = activation / act_norm
    candidates = fetched[:, K:].astype(jnp.float32)
    scores = jnp.einsum("qf,qcf->qc", unit_vec, candidates)
    slopes = jax.nn.sigmoid(scores[:, 1:] - scores[:, :1] + MARGIN)
    slope_sum = jnp.sum(slopes, axis=1, keepdims=True)
    grad_unit = jnp.einsum("qn,qnf->qf", slopes, candidates[:, 1:]) - slope_sum * candidates[:, 0]
    grad_act = (
        grad_unit - unit_vec * jnp.sum(unit_vec * grad_unit, axis=1, keepdims=True)
    ) / act_norm
    grad_pre = (grad_act * gate_value * (1.0 + preact * (1.0 - gate_value))).astype(jnp.bfloat16)
    return (joined, grad_pre, shares, slopes, slope_sum, unit_vec)


def row_cotangents(grad_pre, weight, shares, slopes, slope_sum, unit_vec, feat_dim):
    grad_joined = jnp.dot(grad_pre, weight.T, preferred_element_type=jnp.float32)
    grad_self = grad_joined[:, :feat_dim]
    grad_neigh = shares[:, :, None] * grad_joined[:, None, feat_dim:]
    grad_pos = -slope_sum[:, :, None] * unit_vec[:, None, :]
    grad_neg = slopes[:, :, None] * unit_vec[:, None, :]
    row_terms = jnp.concatenate([grad_neigh, grad_pos, grad_neg], axis=1).astype(jnp.bfloat16)
    return (grad_self, row_terms)


def sum_weights(grad_part):
    return lax.psum_scatter(grad_part, ("shard", "rep"), scatter_dimension=0, tiled=True)


def local(table, self_feat, weight, owners, item_rows, importance):
    shard_count = lax.axis_size("shard")
    owned_rows = table.shape[0]
    feat_dim = table.shape[1]
    query_count = self_feat.shape[0]
    slot_count = item_rows.shape[1]
    request_count = query_count * slot_count
    capacity = (2 * request_count + shard_count - 1) // shard_count
    owner_ids = owners[:, :, 0].reshape(-1)
    local_rows = item_rows.reshape(-1)
    owner_hot = (owner_ids[:, None] == jnp.arange(shard_count, dtype=jnp.int32)[None, :]).astype(
        jnp.int32
    )
    before_count = jnp.cumsum(owner_hot, axis=0) - owner_hot
    position = jnp.sum(before_count * owner_hot, axis=1)
    bucket_slot = owner_ids * capacity + position
    request_ids = jnp.zeros((shard_count * capacity,), jnp.int32).at[bucket_slot].set(local_rows)
    request_ids = request_ids.reshape(shard_count, capacity)
    asked_ids = lax.all_to_all(request_ids, "shard", split_axis=0, concat_axis=0, tiled=True)
    found = table[asked_ids]
    returned = lax.all_to_all(found, "shard", split_axis=0, concat_axis=0, tiled=True)
    fetched_rows = returned.reshape(shard_count * capacity, feat_dim)[bucket_slot]
    fetched = fetched_rows.reshape(query_count, slot_count, feat_dim)
    joined, grad_pre, shares, slopes, slope_sum, unit_vec = forward_backward(
        fetched, self_feat, weight, importance
    )
    grad_part = jnp.dot(joined.T, grad_pre, preferred_element_type=jnp.float32)
    grad_self, row_terms = row_cotangents(
        grad_pre, weight, shares, slopes, slope_sum, unit_vec, feat_dim
    )
    send_rows = (
        jnp.zeros((shard_count * capacity, feat_dim), jnp.bfloat16)
        .at[bucket_slot]
        .set(row_terms.reshape(request_count, feat_dim))
    )
    send_rows = send_rows.reshape(shard_count, capacity, feat_dim)
    received = lax.all_to_all(send_rows, "shard", split_axis=0, concat_axis=0, tiled=True)
    item_hot = (
        jnp.arange(owned_rows, dtype=jnp.int32)[:, None] == asked_ids.reshape(-1)[None, :]
    ).astype(jnp.bfloat16)
    owner_grad = jnp.dot(
        item_hot,
        received.reshape(shard_count * capacity, feat_dim),
        preferred_element_type=jnp.float32,
    )
    grad_table = lax.psum_scatter(owner_grad, "rep", scatter_dimension=0, tiled=True)
    grad_weight = sum_weights(grad_part)
    return (grad_self, grad_weight, grad_table)


def solution(mesh):
    in_specs = (
        P("shard", None),
        P(("shard", "rep"), None),
        P(),
        P(("shard", "rep"), None, None),
        P(("shard", "rep"), None),
        P(("shard", "rep"), None),
    )
    out_specs = (P(("shard", "rep"), None), P(("shard", "rep"), None), P(("shard", "rep"), None))
    return jax.shard_map(local, mesh=mesh, in_specs=in_specs, out_specs=out_specs, check_vma=False)
```

profile of v0, /device:TPU:1, one launch (start us, length us, event | category | flops | bytes accessed | tf_op | source)
XLA Modules:
  0.0 1535.7 jit_solution(17283026679390156905)
XLA Ops:
  7.2 0.8 reshape.148
  8.0 0.5 broadcast.115
  8.5 1.4 fusion.28
  10.1 1.5 reduce-window.6
  11.6 0.3 slice_reduce_fusion
  12.1 4.1 scatter_custom_fusion
  16.3 22.3 %all_to_all.22 = s32[64,1,17]{2,1,0:T(1,128)S(1)} all-to-all(s32[64,1,17]{2,1,0:T(1,128)S(1)} %bitcast.57), channel_id=1, replica_groups=mesh['shard'=64,'rep'=4] {'shard'}, dimensions={0} | all-to-all | bytes 8704 | tf_op jit(solution)/shard_map/all_to_all | solution.py:68
  38.8 4.4 gather_fusion
  43.2 2.5 reshape.129
  45.7 5.8 all-to-all-start.1
  51.7 72.5 %all-to-all-done.1 = bf16[64,17,1024]{2,1,0:T(8,128)(2,1)} async-done(((bf16[64,17,1024]{2,1,0:T(8,128)(2,1)}), bf16[64,17,1024]{2,1,0:T(8,128)(2,1)}, u32[]{:S(2)}, u32[]{:S(2)}) %all-to-all-start.1) | async-done | bytes 2228256 | tf_op jit(solution)/shard_map/all_to_all | solution.py:70
  124.2 3.0 reshape.122
  127.2 2.8 gather_fusion.1
  130.0 0.3 reshape.123
  130.4 0.3 fusion.2
  130.7 3.0 multiply_reduce_fusion.1
  133.9 0.2 fusion.4
  134.6 0.2 multiply_reduce_fusion
  134.9 3.4 fusion.32
  138.3 0.6 fusion.31
  139.2 0.2 pad_maximum_fusion
  139.4 0.3 reshape.156
  139.8 6.4 scatter_custom_fusion.1
  146.2 2.5 reshape.124
  148.7 6.5 all-to-all-start.2
  155.2 0.7 reduce.15
  156.1 71.6 %all-to-all-done.2 = bf16[64,17,1024]{2,1,0:T(8,128)(2,1)S(1)} async-done(((bf16[64,17,1024]{2,1,0:T(8,128)(2,1)}), bf16[64,17,1024]{2,1,0:T(8,128)(2,1)S(1)}, u32[]{:S(2)}, u32[]{:S(2)}) %all-to-all-start.2) | async-done | bytes 2228256 | tf_op jit(solution)/shard_map/all_to_all | solution.py:86
  227.7 2.3 reshape.125
  230.0 2.8 fusion.10
  232.8 4.5 fusion.15
  237.4 13.5 reduce-scatter.5.cloned.1.call-done
  250.9 1278.0 %reduce-scatter.3.cloned.1.call-done = f32[8,1024]{1,0:T(8,128)} async-done(((f32[2048,1024]{1,0:T(8,128)}), f32[8,1024]{1,0:T(8,128)}) %reduce-scatter.3.cloned.1.call-update) | async-done | bytes 32784 | tf_op jit(solution)/shard_map/reduce_scatter | solution.py:47
  (42 shorter events, 2.2 us)
Async XLA Ops:
  7.2 31.6 %copy-start = (bf16[32,1024]{1,0:T(8,128)(2,1)S(1)}, bf16[32,1024]{1,0:T(8,128)(2,1)}, u32[]{:S(2)}) copy-start(bf16[32,1024]{1,0:T(8,128)(2,1)} %param.6) | copy-start | bytes 196612
  45.7 5.8 copy-start.2
  45.7 78.5 %all-to-all-start.1 = ((bf16[64,17,1024]{2,1,0:T(8,128)(2,1)}), bf16[64,17,1024]{2,1,0:T(8,128)(2,1)}, u32[]{:S(2)}, u32[]{:S(2)}) async-start(bf16[64,17,1024]{2,1,0:T(8,128)(2,1)} %reshape.129), calls=%async_computation.1 | async-start | bytes 6291456 | tf_op jit(solution)/shard_map/all_to_all | solution.py:70
  130.0 0.7 copy-start.1
  148.7 79.1 %all-to-all-start.2 = ((bf16[64,17,1024]{2,1,0:T(8,128)(2,1)}), bf16[64,17,1024]{2,1,0:T(8,128)(2,1)S(1)}, u32[]{:S(2)}, u32[]{:S(2)}) async-start(bf16[64,17,1024]{2,1,0:T(8,128)(2,1)} %reshape.124), calls=%async_computation.3 | async-start | bytes 6291456 | tf_op jit(solution)/shard_map/all_to_all | solution.py:86
  155.2 95.7 %reduce-scatter.5.cloned.1.call-start = ((), (), s32[]{:S(2)}) async-start(), calls=%async_computation.6 | async-start | bytes 163840 | tf_op jit(solution)/shard_map/reduce_scatter | solution.py:95
  232.8 1296.1 %reduce-scatter.3.cloned.1.call-start = ((), (), s32[]{:S(2)}) async-start(), calls=%async_computation.5 | async-start | bytes 8421376 | tf_op jit(solution)/shard_map/reduce_scatter | solution.py:47
Sparse Core Ops, SparseCore 0:
  232.9 17.9 reduce-scatter.4
  254.1 1274.7 reduce-scatter.2
where the time goes:
time: 1540 us
  waiting for transfers between devices  1440 us (94%)
  local copies, waits for them, and re-layouts  31.7 us (2%)
  blocking collectives  22.3 us (1%)
    reduce_scatter x1, waiting for transfers between devices, sum_weights(): lax.psum_scatter(grad_part, ('shard', 'rep'), scatter_dimension=0, tiled=...  1280 us
    all_to_all x1, waiting for transfers between devices, local(): lax.all_to_all(found, 'shard', split_axis=0, concat_axis=0, tiled=True)  72.5 us
    all_to_all x1, waiting for transfers between devices, local(): lax.all_to_all(send_rows, 'shard', split_axis=0, concat_axis=0, tiled=True)  71.6 us
  transfers between devices with their start and end apart: 4, of which 4 were waited for; matrix products, arithmetic and copies ran while one was open for 0% of the time, Pallas kernels for 0%

commit v1 on v0

v1 whole, which is shorter than its diff:
```python
import jax
import jax.numpy as jnp
from jax import lax
from jax.experimental import pallas as pl
from jax.experimental.pallas import tpu as pltpu
from jax.sharding import PartitionSpec as P

MESH = pl.DeviceIdType.MESH
MARGIN = 0.5
EPS = 1e-06
K = 50
C = 17
NZ, NY, NX = 8, 4, 4
NB = NZ * NY
NE = NY * NX
Q = 8
G = NZ * Q
L = 128
ITEMS = 2048
HALF = ITEMS // 2
F32, BF16 = jnp.float32, jnp.bfloat16
QI_, SF_, TA_, TP_, PO_, PC_, GP_, HW_, HT_, EW_, ET_, OW_, OT_ = range(13)


def tdot(a, b):
    return lax.dot_general(a, b, (((0,), (0,)), ((), ())), preferred_element_type=F32)


def ntdot(a, b):
    return lax.dot_general(a, b, (((1,), (1,)), ((), ())), preferred_element_type=F32)


def kernel(
    tab, sf, qin, w_hbm, o_self, o_w, o_t,
    t_all, qi, sf_all, pooled, parts, gpre, hot, id_b, imp_b, w_b, cand, w2,
    wf, wbp, wtop, rw, rt, hws, hwr, hts, htr, esw, est, eww, ewt, rsw, rst, oww, owt, gself,
    sems, wsem,
):
    s = lax.axis_index("shard")
    x = lax.axis_index("rep")
    c = lax.rem(s, 2)
    b = lax.div(s, 2)
    z = lax.div(b, NY)
    y = lax.rem(b, NY)
    e = y * NX + x
    partner = (b * 2 + 1 - c, x)

    def on_plane(off):
        other = lax.rem(b + off, NB)
        return other, (other * 2 + c, x)

    def on_line(off):
        other = lax.rem(z + off, NZ)
        return other, ((other * NY + y) * 2 + c, x)

    def on_face(off):
        other = lax.rem(e + off, NE)
        return other, ((z * NY + lax.div(other, NX)) * 2 + c, lax.rem(other, NX))

    def send(src, dst, row, to):
        pltpu.make_async_remote_copy(
            src_ref=src, dst_ref=dst, send_sem=sems.at[row, 0], recv_sem=sems.at[row, 1],
            device_id=to, device_id_type=MESH,
        ).start()

    def done(ref, row):
        return pltpu.make_async_remote_copy(
            src_ref=ref, dst_ref=ref, send_sem=sems.at[row, 0], recv_sem=sems.at[row, 1],
            device_id=partner, device_id_type=MESH,
        )

    def each(n, body):
        def step(i, carry):
            body(i)
            return carry
        lax.fori_loop(1, n, step, 0)

    zcol = pl.ds(pl.multiple_of(z * L, L), L)
    zrow = pl.ds(pl.multiple_of(z * L, L), L)
    loads = [
        pltpu.make_async_copy(w_hbm.at[:, zcol], wf, wsem.at[0]),
        pltpu.make_async_copy(
            w_hbm.at[pl.ds(pl.multiple_of(1024 + z * L, L), L), :], wbp, wsem.at[1]),
        pltpu.make_async_copy(w_hbm.at[pl.ds(0, 1024), :], wtop, wsem.at[2]),
    ]
    for load in loads:
        load.start()

    bar = pltpu.get_barrier_semaphore()

    def greet(to):
        pl.semaphore_signal(bar, inc=1, device_id=to, device_id_type=MESH)

    each(NB, lambda i: greet(on_plane(i)[1]))
    each(NE, lambda i: greet(on_face(i)[1]))
    greet(partner)
    qi[z] = qin[...]
    own_self = sf[...].astype(F32)
    sf_all[z] = jnp.concatenate([own_self[:, :512], own_self[:, 512:]], axis=0).astype(BF16)
    t_all[c, b] = tab[:, zcol]
    pl.semaphore_wait(bar, NB - 1 + NE - 1 + 1)

    each(NZ, lambda i: send(qi.at[z], qi.at[z], QI_, on_line(i)[1]))

    def send_table(i):
        other, to = on_plane(i)
        cols = pl.ds(pl.multiple_of(lax.div(other, NY) * L, L), L)
        send(tab.at[:, cols], t_all.at[c, b], TA_, to)

    each(NB, send_table)
    each(NZ, lambda i: send(sf_all.at[z], sf_all.at[z], SF_, on_line(i)[1]))

    done(qi.at[pl.ds(0, NZ - 1)], QI_).wait_recv()
    ids = qi[:, 0:Q, :].reshape(G, L)
    imp = qi[:, Q:2 * Q, :].reshape(G, L).astype(F32)
    for k in range(K + C):
        id_b[k] = jnp.broadcast_to(ids[:, k:k + 1], (G, L))
    for k in range(K):
        imp_b[k] = jnp.broadcast_to(imp[:, k:k + 1], (G, L))
    inv = 1.0 / jnp.sum(imp, axis=1, keepdims=True)
    lane = lax.broadcasted_iota(jnp.int32, (G, L), 1)

    def hot_chunk(h, carry):
        here = lane + h * L
        cols = pl.ds(pl.multiple_of(h * L, L), L)

        def add(k, acc):
            return acc + jnp.where(id_b[k] == here, imp_b[k], 0.0)

        acc = lax.fori_loop(0, K, add, jnp.zeros((G, L), F32), unroll=10)
        hot[0, :, cols] = acc.astype(BF16)
        for k in range(C):
            hot[1 + k, :, cols] = jnp.where(id_b[K + k] == here, 1.0, 0.0).astype(BF16)
        return carry

    lax.fori_loop(0, ITEMS // L, hot_chunk, 0)

    loads[0].wait()
    done(sf_all.at[pl.ds(0, NZ - 1)], SF_).wait_recv()
    self2 = sf_all[...].reshape(2 * G, 512)
    w_self = jnp.concatenate([wf[0:512, :], wf[512:1024, :]], axis=1)
    pre2 = jnp.dot(self2, w_self, preferred_element_type=F32).reshape(NZ, 2, Q, 2 * L)
    pre_self = (pre2[:, 0, :, :L] + pre2[:, 1, :, L:]).reshape(G, L)

    done(t_all.at[c, pl.ds(0, NB - 1)], TA_).wait_recv()
    send(t_all.at[c], t_all.at[c], TP_, partner)
    done(t_all.at[1 - c], TP_).wait_recv()

    rows = t_all[...].reshape(ITEMS, L)
    mine = jnp.dot(hot[0], rows, preferred_element_type=F32) * inv
    pooled[z] = mine.astype(BF16)
    each(NZ, lambda i: send(pooled.at[z], pooled.at[z], PO_, on_line(i)[1]))
    cand[...] = jnp.dot(
        hot[1:1 + C].reshape(C * G, ITEMS), rows, preferred_element_type=F32
    ).reshape(C, G, L)

    done(pooled.at[pl.ds(0, NZ - 1)], PO_).wait_recv()
    pool_all = jnp.concatenate([pooled[f] for f in range(NZ)], axis=1)
    pre = pre_self + jnp.dot(pool_all, wf[1024:2048, :], preferred_element_type=F32)
    gate = jax.nn.sigmoid(pre)
    act = pre * gate
    place = 32 * lax.rem(lax.div(lax.broadcasted_iota(jnp.int32, (G, L), 0), Q), 4)
    where_at = lane - place
    acc = jnp.where(where_at == C, jnp.sum(act * act, axis=1, keepdims=True), 0.0)
    for k in range(C):
        acc = jnp.where(where_at == k, jnp.sum(act * cand[k], axis=1, keepdims=True), acc)
    acc = acc.reshape(2, 4, Q, L)
    parts[z] = (acc[:, 0] + acc[:, 1] + acc[:, 2] + acc[:, 3]).reshape(2 * Q, L)
    each(NZ, lambda i: send(parts.at[z], parts.at[z], PC_, on_line(i)[1]))
    done(parts.at[pl.ds(0, NZ - 1)], PC_).wait_recv()
    total = parts[0]
    for f in range(1, NZ):
        total = total + parts[f]
    sums = jnp.concatenate(
        [total[(j // 4) * Q:(j // 4 + 1) * Q, 32 * (j % 4):32 * (j % 4) + 32] for j in range(NZ)],
        axis=0,
    )
    norm = jnp.sqrt(sums[:, C:C + 1] + EPS)
    score = sums / norm
    lane32 = lax.broadcasted_iota(jnp.int32, (G, 32), 1)
    negative = (lane32 >= 1) & (lane32 < C)
    slope = jnp.where(negative, jax.nn.sigmoid(score - score[:, 0:1] + MARGIN), 0.0)
    slope_sum = jnp.sum(slope, axis=1, keepdims=True)
    coef = jnp.where(lane32 == 0, -slope_sum, slope)
    along = jnp.sum(coef * score, axis=1, keepdims=True)
    grad_unit = jnp.zeros((G, L), F32)
    for k in range(C):
        wk = jnp.broadcast_to(coef[:, k:k + 1], (G, L))
        w_b[k] = wk
        grad_unit = grad_unit + wk * cand[k]
    unit = act / norm
    grad_act = (grad_unit - unit * along) / norm
    grad_pre = grad_act * gate * (1.0 + pre * (1.0 - gate))
    gp16 = grad_pre.astype(BF16)
    gpre[z] = gp16
    each(NZ, lambda i: send(gpre.at[z], gpre.at[z], GP_, on_line(i)[1]))

    blank = jnp.zeros((Q, L), F32)
    gp32 = gp16.astype(F32)
    pieces = []
    for j in range(NZ):
        part = gp32[j * Q:(j + 1) * Q]
        pieces.append(jnp.concatenate([part, blank], axis=1))
        pieces.append(jnp.concatenate([blank, part], axis=1))
    gp2 = jnp.concatenate(pieces, axis=0).astype(BF16)
    gw_self = tdot(self2, gp2)
    rw[0:2] = gw_self[:, :L].reshape(2, NY, 2, NX, Q, L)
    rw[2:4] = gw_self[:, L:].reshape(2, NY, 2, NX, Q, L)
    rw[4:8] = tdot(pool_all, gp16).reshape(4, NY, 2, NX, Q, L)
    for k in range(NE):
        hws[k] = rw[:, k // NX, 1 - c, k % NX].reshape(NZ * Q, L).astype(BF16)
    send(hws, hwr, HW_, partner)

    def w2_chunk(h, carry):
        here = lane + h * L
        cols = pl.ds(pl.multiple_of(h * L, L), L)
        acc = jnp.zeros((G, L), F32)
        for k in range(C):
            acc = acc + jnp.where(id_b[K + k] == here, w_b[k], 0.0)
        w2[:, cols] = acc.astype(BF16)
        return carry

    lax.fori_loop(0, ITEMS // L, w2_chunk, 0)
    done(hwr, HW_).wait_recv()
    for k in range(NE):
        own = rw[:, k // NX, c, k % NX].reshape(NZ * Q, L)
        esw[k] = (own + hwr[k].astype(F32)).astype(BF16)
    each(NE, lambda i: send(esw.at[on_face(i)[0]], eww.at[e], EW_, on_face(i)[1]))
    eww[e] = esw[e]

    rt[...] = tdot(w2[...], unit.astype(BF16)).reshape(2, NZ, NY, NX, Q, L)

    done(gpre.at[pl.ds(0, NZ - 1)], GP_).wait_recv()
    gp_all = jnp.concatenate([gpre[f] for f in range(NZ)], axis=1)
    loads[1].wait()
    gps = (ntdot(gp_all, wbp[...]) * inv).astype(BF16)
    rt[...] += tdot(hot[0], gps).reshape(2, NZ, NY, NX, Q, L)
    for k in range(NE):
        hts[k] = rt[1 - c, :, k // NX, k % NX].reshape(NZ * Q, L).astype(BF16)
    send(hts, htr, HT_, partner)
    loads[2].wait()
    gself[...] = ntdot(gp_all, wtop[...])
    o_self[...] = gself[pl.ds(pl.multiple_of(z * Q, Q), Q), :]

    done(htr, HT_).wait_recv()
    for k in range(NE):
        own = rt[c, :, k // NX, k % NX].reshape(NZ * Q, L)
        est[k] = (own + htr[k].astype(F32)).astype(BF16)
    each(NE, lambda i: send(est.at[on_face(i)[0]], ewt.at[e], ET_, on_face(i)[1]))
    ewt[e] = est[e]

    def finish(got, row, summed, final, last):
        done(got.at[pl.ds(0, NE - 1)], row).wait_recv()
        acc = got[0].astype(F32)
        for k in range(1, NE):
            acc = acc + got[k].astype(F32)
        summed[...] = acc.reshape(NZ, Q, L)
        final[z] = summed[z]
        each(NZ, lambda i: send(summed.at[on_line(i)[0]], final.at[z], last, on_line(i)[1]))

    def write(final, last, out):
        done(final.at[pl.ds(0, NZ - 1)], last).wait_recv()
        for f in range(NZ):
            out[:, f * L:(f + 1) * L] = final[f]

    finish(eww, EW_, rsw, oww, OW_)
    finish(ewt, ET_, rst, owt, OT_)
    write(oww, OW_, o_w)
    write(owt, OT_, o_t)

    for ref, row in (
        (qi.at[pl.ds(0, NZ - 1)], QI_), (sf_all.at[pl.ds(0, NZ - 1)], SF_),
        (t_all.at[c, pl.ds(0, NB - 1)], TA_), (t_all.at[c], TP_),
        (pooled.at[pl.ds(0, NZ - 1)], PO_), (parts.at[pl.ds(0, NZ - 1)], PC_),
        (gpre.at[pl.ds(0, NZ - 1)], GP_), (hws, HW_), (hts, HT_),
        (esw.at[pl.ds(0, NE - 1)], EW_), (est.at[pl.ds(0, NE - 1)], ET_),
        (rsw.at[pl.ds(0, NZ - 1)], OW_), (rst.at[pl.ds(0, NZ - 1)], OT_),
    ):
        done(ref, row).wait_send()


def local(table, self_feat, weight, owners, item_rows, importance):
    own = owners[:, :, 0]
    at = (own % 2) * HALF + (own // 2) * 32 + item_rows
    qin = jnp.concatenate(
        [jnp.pad(at, ((0, 0), (0, L - K - C))), jnp.pad(importance, ((0, 0), (0, L - K)))], axis=0
    )
    vmem = pl.BlockSpec(memory_space=pltpu.VMEM)
    out = jax.ShapeDtypeStruct((Q, 1024), F32)
    V = pltpu.VMEM
    return pl.pallas_call(
        kernel,
        out_shape=(out, out, out),
        in_specs=[vmem, vmem, vmem, pl.BlockSpec(memory_space=pl.ANY)],
        out_specs=(vmem, vmem, vmem),
        scratch_shapes=[
            V((2, NB, 32, L), BF16),
            V((NZ, 2 * Q, L), jnp.int32),
            V((NZ, 2 * Q, 512), BF16),
            V((NZ, G, L), BF16),
            V((NZ, 2 * Q, L), F32),
            V((NZ, G, L), BF16),
            V((1 + C, G, ITEMS), BF16),
            V((K + C, G, L), jnp.int32),
            V((K, G, L), F32),
            V((C, G, L), F32),
            V((C, G, L), F32),
            V((G, ITEMS), BF16),
            V((ITEMS, L), BF16),
            V((L, 1024), BF16),
            V((1024, 1024), BF16),
            V((NZ, NY, 2, NX, Q, L), F32),
            V((2, NZ, NY, NX, Q, L), F32),
            V((NE, G, L), BF16),
            V((NE, G, L), BF16),
            V((NE, G, L), BF16),
            V((NE, G, L), BF16),
            V((NE, G, L), BF16),
            V((NE, G, L), BF16),
            V((NE, G, L), BF16),
            V((NE, G, L), BF16),
            V((NZ, Q, L), F32),
            V((NZ, Q, L), F32),
            V((NZ, Q, L), F32),
            V((NZ, Q, L), F32),
            V((G, 1024), F32),
            pltpu.SemaphoreType.DMA((13, 2)),
            pltpu.SemaphoreType.DMA((3,)),
        ],
        compiler_params=pltpu.CompilerParams(
            collective_id=0, has_side_effects=True, vmem_limit_bytes=48 * 1024 * 1024
        ),
    )(table, self_feat, qin, weight)


def solution(mesh):
    both = ("shard", "rep")
    in_specs = (
        P("shard", None), P(both, None), P(), P(both, None, None), P(both, None), P(both, None),
    )
    out_specs = (P(both, None), P(both, None), P(both, None))
    return jax.shard_map(local, mesh=mesh, in_specs=in_specs, out_specs=out_specs, check_vma=False)
```

time: 1540 us -> 63.5 us (0.04)
  waiting for transfers between devices: 1440 us -> 0 us
  Pallas kernels: 0 us -> 55.6 us
  local copies, waits for them, and re-layouts: 31.7 us -> 5.59 us
  blocking collectives: 22.3 us -> 0 us
    reduce_scatter x2 -> x0, waiting for transfers between devices: 1290 us -> none  [the longest x1 1280 us: sum_weights(): lax.psum_scatter(grad_part, ('shard', 'rep'), scatter_dimension=0, tiled=...]
    all_to_all x2 -> x0, waiting for transfers between devices: 144 us -> none  [the longest x1 72.5 us: local(): lax.all_to_all(found, 'shard', split_axis=0, concat_axis=0, tiled=True)]
    pallas_call x0 -> x1, Pallas kernels: none -> 55.6 us  [local(): pl.pallas_call(kernel, out_shape=(out, out, out), in_specs=[vmem, vmem, v...]
    all_to_all x1 -> x0, blocking collectives: 22.3 us -> none  [local(): lax.all_to_all(request_ids, 'shard', split_axis=0, concat_axis=0, tiled=T...]
  transfers between devices with their start and end apart: 4 -> 0, of which waited for: 4 -> 0; matrix products, arithmetic and copies ran while one was open for 0% -> 0% of each run, Pallas kernels for 0% -> 0%
where the time goes in v1:
time: 63.5 us; the launch traced here: 63.2 us
  Pallas kernels  55.6 us (88%)
  local copies, waits for them, and re-layouts  5.59 us (9%)
  other arithmetic  1.41 us (2%)
  between operations  0.64 us (1%)
    pallas_call x1, Pallas kernels, local(): pl.pallas_call(kernel, out_shape=(out, out, out), in_specs=[vmem, vmem, v...  55.6 us
    unnamed x9, local copies, waits for them, and re-layouts  5.59 us

profile of v1, /device:TPU:1, one launch (start us, length us, event | category | flops | bytes accessed | tf_op | source)
XLA Modules:
  0.0 63.2 jit_solution(14463893965500589655)
XLA Ops:
  0.6 0.7 %fusion.2 = s32[8,67]{1,0:T(8,128)S(1)} fusion(s32[8,67]{1,0:T(8,128)} %param.10, s32[8,67]{1,0:T(8,128)} %bitcast.1), kind=kLoop, calls=%fused_computation.8 | loop fusion | flops 12328 | bytes 6432 | tf_op jit(solution)/shard_map/add | solution.py:284
  1.3 0.7 %pad_add_fusion.qin = s32[16,128]{1,0:T(8,128)S(1)} fusion(s32[8,50]{1,0:T(8,128)} %param.11, s32[8,67]{1,0:T(8,128)S(1)} %fusion.2), kind=kLoop, calls=%fused_computation | loop fusion | flops 2048 | bytes 11936 | tf_op jit(solution)/shard_map/concatenate | solution.py:285
  2.0 0.0 copy-start
  2.0 2.2 %copy-done = bf16[2048,1024]{1,0:T(8,128)(2,1)S(1)} copy-done((bf16[2048,1024]{1,0:T(8,128)(2,1)S(1)}, bf16[2048,1024]{1,0:T(8,128)(2,1)}, u32[]{:S(2)}) %copy-start) | copy-done | bytes 4194328
  4.2 0.0 copy-start.1
  4.2 0.8 %copy-done.1 = bf16[32,1024]{1,0:T(8,128)(2,1)S(1)} copy-done((bf16[32,1024]{1,0:T(8,128)(2,1)S(1)}, bf16[32,1024]{1,0:T(8,128)(2,1)}, u32[]{:S(2)}) %copy-start.1) | copy-done | bytes 65560
  5.1 0.0 copy-start.2
  5.1 0.7 %copy-done.2 = bf16[8,1024]{1,0:T(8,128)(2,1)S(1)} copy-done((bf16[8,1024]{1,0:T(8,128)(2,1)S(1)}, bf16[8,1024]{1,0:T(8,128)(2,1)}, u32[]{:S(2)}) %copy-start.2) | copy-done | bytes 16408
  5.8 55.6 %shard_map.85 = (f32[8,1024]{1,0:T(8,128)S(1)}, f32[8,1024]{1,0:T(8,128)S(1)}, f32[8,1024]{1,0:T(8,128)S(1)}) custom-call(bf16[32,1024]{1,0:T(8,128)(2,1)S(1)} %copy-done.1, bf16[8,1024]{1,0:T(8,128)(2,1)S(1)} %copy-done.2, s32[16,128]{1,0:T(8,128)S(1)} %pad_add_fusion.qin, bf16[2048,1024]{1,0:T(8,128)(2,1)S(1)} %copy-done), custom_call_target="tpu_custom_call" | custom-call | tf_op jit(solution)/shard_map/pallas_call | solution.py:291
  61.4 0.6 copy.12
  62.0 0.6 copy.13
  62.6 0.6 copy.14
Async XLA Ops:
  2.0 2.2 %copy-start = (bf16[2048,1024]{1,0:T(8,128)(2,1)S(1)}, bf16[2048,1024]{1,0:T(8,128)(2,1)}, u32[]{:S(2)}) copy-start(bf16[2048,1024]{1,0:T(8,128)(2,1)} %w_hbm.1) | copy-start | bytes 12582916
  4.2 0.8 %copy-start.1 = (bf16[32,1024]{1,0:T(8,128)(2,1)S(1)}, bf16[32,1024]{1,0:T(8,128)(2,1)}, u32[]{:S(2)}) copy-start(bf16[32,1024]{1,0:T(8,128)(2,1)} %tab.1) | copy-start | bytes 196612
  5.1 0.7 %copy-start.2 = (bf16[8,1024]{1,0:T(8,128)(2,1)S(1)}, bf16[8,1024]{1,0:T(8,128)(2,1)}, u32[]{:S(2)}) copy-start(bf16[8,1024]{1,0:T(8,128)(2,1)} %sf.1) | copy-start | bytes 49156

commit v2 on v1

v2 whole, which is shorter than its diff:
```python
import jax
import jax.numpy as jnp
from jax import lax
from jax.experimental import pallas as pl
from jax.experimental.pallas import tpu as pltpu
from jax.sharding import PartitionSpec as P

MESH = pl.DeviceIdType.MESH
MARGIN = 0.5
EPS = 1e-06
K = 50
C = 17
NZ, NY, NX = 8, 4, 4
NB = NZ * NY
NE = NY * NX
Q = 8
G = NZ * Q
L = 128
ITEMS = 2048
HALF = ITEMS // 2
F32, BF16 = jnp.float32, jnp.bfloat16
QI_, SF_, TP_, PO_, PC_, GP_, PS_ = range(7)
HALF_, FACE_, LINE_ = 7, 10, 13
TZ_, TY_ = 16, 24


def tdot(a, b):
    return lax.dot_general(a, b, (((0,), (0,)), ((), ())), preferred_element_type=F32)


def ntdot(a, b):
    return lax.dot_general(a, b, (((1,), (1,)), ((), ())), preferred_element_type=F32)


def kernel(
    tab_hbm, sf_hbm, own_hbm, row_hbm, imp_hbm, w_hbm, o_self, o_w, o_t,
    tab, sf, own_in, row_in, imp_in,
    t_all, qi, sf_all, ps_out, ps_in, pooled, parts, gsend, grecv, hot, id_b, cand, w2,
    at_hi, at_lo, cand_hi, cand_lo,
    wf, wtop, wbot, rx, rw, ry, half_out, half_in, face_out, face_in, line_out, line_in,
    sems, wsem,
):
    s = lax.axis_index("shard")
    x = lax.axis_index("rep")
    c = s & 1
    b = s >> 1
    z = b >> 2
    y = b & (NY - 1)
    e = y * NX + x
    partner = (b * 2 + 1 - c, x)

    def on_line(off):
        other = (z + off) & (NZ - 1)
        return other, ((other * NY + y) * 2 + c, x)

    def on_face(off):
        other = (e + off) & (NE - 1)
        return other, ((z * NY + (other >> 2)) * 2 + c, (other & (NX - 1)))

    def send(src, dst, row, to):
        pltpu.make_async_remote_copy(
            src_ref=src, dst_ref=dst, send_sem=sems.at[row, 0], recv_sem=sems.at[row, 1],
            device_id=to, device_id_type=MESH,
        ).start()

    def done(ref, row):
        return pltpu.make_async_remote_copy(
            src_ref=ref, dst_ref=ref, send_sem=sems.at[row, 0], recv_sem=sems.at[row, 1],
            device_id=partner, device_id_type=MESH,
        )

    def each(n, body):
        def step(i, carry):
            body(i)
            return carry
        lax.fori_loop(1, n, step, 0)

    zcol = pl.ds(pl.multiple_of(z * L, L), L)
    loads = [
        pltpu.make_async_copy(w_hbm.at[pl.ds(1024, 1024), zcol], wf, wsem.at[0]),
        pltpu.make_async_copy(w_hbm.at[pl.ds(0, 1024), :], wtop, wsem.at[1]),
        pltpu.make_async_copy(w_hbm.at[pl.ds(1024, 1024), :], wbot, wsem.at[2]),
    ]
    small = [
        pltpu.make_async_copy(src, dst, wsem.at[3 + i])
        for i, (src, dst) in enumerate((
            (own_hbm, own_in), (row_hbm, row_in), (imp_hbm, imp_in), (tab_hbm, tab), (sf_hbm, sf)))
    ]
    for load in small + loads:
        load.start()

    bar = pltpu.get_barrier_semaphore()

    def greet(to):
        pl.semaphore_signal(bar, inc=1, device_id=to, device_id_type=MESH)

    each(NZ, lambda i: greet(on_line(i)[1]))
    each(NE, lambda i: greet(on_face(i)[1]))
    greet(partner)
    for load in small:
        load.wait()
    own = own_in[...]
    at = (own & 1) * HALF + (own >> 1) * 32 + row_in[...]
    qi[z] = jnp.zeros((Q, L), jnp.int32)
    qi[z, :, 0:K + C] = at
    qi[z, :, K + C:2 * K + C] = imp_in[...]
    own_self = sf[...].astype(F32)
    sf_all[z] = jnp.concatenate([own_self[:, :512], own_self[:, 512:]], axis=0).astype(BF16)
    t_all[c, b] = tab[:, zcol]
    pl.semaphore_wait(bar, NZ - 1 + NE - 1 + 1)

    each(NZ, lambda i: send(qi.at[z], qi.at[z], QI_, on_line(i)[1]))

    for k in (4, 3, 5, 2, 6, 1, 7):
        to_z = (z - k) & (NZ - 1)
        cols = pl.ds(pl.multiple_of(to_z * L, L), L)
        send(tab.at[:, cols], t_all.at[c, b], TZ_ + k, ((to_z * NY + y) * 2 + c, x))

    def pass_on(k):
        at = t_all.at[c, ((z + k) & (NZ - 1)) * NY + y]
        for dy in range(1, NY):
            send(at, at, TY_ + k, ((z * NY + ((y + dy) & (NY - 1))) * 2 + c, x))
        send(at, at, TP_, partner)

    pass_on(0)
    loads[1].wait()
    own_pre = jnp.dot(sf[...], wtop[...], preferred_element_type=F32)
    for f in range(NZ):
        ps_out[f] = own_pre[:, f * L:(f + 1) * L]
    each(NZ, lambda i: send(ps_out.at[on_line(i)[0]], ps_in.at[z], PS_, on_line(i)[1]))
    ps_in[z] = ps_out[z]
    for k in (1, 7, 2, 6, 3, 5, 4):
        done(t_all.at[c, b], TZ_ + k).wait_recv()
        pass_on(k)

    done(qi.at[pl.ds(0, NZ - 1)], QI_).wait_recv()
    ids = qi[...].reshape(G, L)
    imp = ids.astype(F32)
    lane = lax.broadcasted_iota(jnp.int32, (G, L), 1)
    query = lax.broadcasted_iota(jnp.int32, (G, L), 0) & (Q - 1)
    weighed = (lane >= K + C) & (lane < 2 * K + C)
    inv = 1.0 / jnp.sum(jnp.where(weighed, imp, 0.0), axis=1, keepdims=True)
    ids_hi = (ids >> 7) * Q + query
    ids_lo = ids & (L - 1)

    def spread(values, k):
        return jnp.broadcast_to(values[:, k:k + 1], (G, L))

    def pair(one, two):
        both = jnp.concatenate([one.reshape(NZ, Q, L), two.reshape(NZ, Q, L)], axis=1)
        return both.astype(BF16)

    def hit(values, k, weight=1.0):
        return jnp.where(spread(values, k) == lane, weight, 0.0)

    def outer(out, hi, lo):
        for m in range(NZ // 2):
            one = tdot(hi[2 * m], lo[2 * m])
            two = tdot(hi[2 * m + 1], lo[2 * m + 1])
            for h in range(ITEMS // L):
                both = jnp.concatenate([one[h * Q:(h + 1) * Q], two[h * Q:(h + 1) * Q]], axis=0)
                out[2 * m * Q:2 * (m + 1) * Q, h * L:(h + 1) * L] = both.astype(BF16)

    for m in range(K // 2):
        k = 2 * m
        at_hi[:, k * Q:(k + 2) * Q] = pair(hit(ids_hi, k), hit(ids_hi, k + 1))
        at_lo[:, k * Q:(k + 2) * Q] = pair(
            hit(ids_lo, k, spread(imp, K + C + k)), hit(ids_lo, k + 1, spread(imp, K + C + k + 1)))
    outer(hot.at[0], at_hi, at_lo)

    for k in (0, 1, 7, 2, 6, 3, 5, 4):
        first = ((z + k) & (NZ - 1)) * NY
        done(t_all.at[c, pl.ds(first, NY - 1)], TY_ + k).wait_recv()
        for dy in range(1, NY):
            at = t_all.at[c, first + ((y + dy) & (NY - 1))]
            send(at, at, TP_, partner)
    done(t_all.at[1 - c], TP_).wait_recv()

    rows = t_all[...].reshape(ITEMS, L)
    mine = jnp.dot(hot[0], rows, preferred_element_type=F32) * inv
    pooled[z] = mine.astype(BF16)
    each(NZ, lambda i: send(pooled.at[z], pooled.at[z], PO_, on_line(i)[1]))
    for k in range(C):
        id_b[k] = spread(ids, K + k)

    def hot_chunk(h, carry):
        here = lane + h * L
        cols = pl.ds(pl.multiple_of(h * L, L), L)
        for k in range(C):
            hot[1 + k, :, cols] = jnp.where(id_b[k] == here, 1.0, 0.0).astype(BF16)
        return carry

    lax.fori_loop(0, ITEMS // L, hot_chunk, 0)
    cand[...] = jnp.dot(
        hot[1:1 + C].reshape(C * G, ITEMS), rows, preferred_element_type=F32
    ).reshape(C, G, L)

    zero = jnp.zeros((G, L), F32)
    for m in range((C + 1) // 2):
        k = K + 2 * m
        last = zero if 2 * m + 1 == C else hit(ids_hi, k + 1)
        cand_hi[:, 2 * m * Q:(2 * m + 2) * Q] = pair(hit(ids_hi, k), last)
    loads[0].wait()
    done(pooled.at[pl.ds(0, NZ - 1)], PO_).wait_recv()
    pool_all = jnp.concatenate([pooled[f] for f in range(NZ)], axis=1)
    done(ps_in.at[pl.ds(0, NZ - 1)], PS_).wait_recv()
    pre = ps_in[...].reshape(G, L) + jnp.dot(pool_all, wf[...], preferred_element_type=F32)
    gate = jax.nn.sigmoid(pre)
    act = pre * gate
    place = 32 * lax.rem(lax.div(lax.broadcasted_iota(jnp.int32, (G, L), 0), Q), 4)
    where_at = lane - place
    acc = jnp.where(where_at == C, jnp.sum(act * act, axis=1, keepdims=True), 0.0)
    for k in range(C):
        acc = jnp.where(where_at == k, jnp.sum(act * cand[k], axis=1, keepdims=True), acc)
    acc = acc.reshape(2, 4, Q, L)
    parts[z] = (acc[:, 0] + acc[:, 1] + acc[:, 2] + acc[:, 3]).reshape(2 * Q, L)
    each(NZ, lambda i: send(parts.at[z], parts.at[z], PC_, on_line(i)[1]))
    each(NZ, lambda i: send(sf_all.at[z], sf_all.at[z], SF_, on_line(i)[1]))
    done(parts.at[pl.ds(0, NZ - 1)], PC_).wait_recv()
    total = parts[0]
    for f in range(1, NZ):
        total = total + parts[f]
    sums = jnp.concatenate(
        [total[(j // 4) * Q:(j // 4 + 1) * Q, 32 * (j % 4):32 * (j % 4) + 32] for j in range(NZ)],
        axis=0,
    )
    norm = jnp.sqrt(sums[:, C:C + 1] + EPS)
    score = sums / norm
    lane32 = lax.broadcasted_iota(jnp.int32, (G, 32), 1)
    negative = (lane32 >= 1) & (lane32 < C)
    slope = jnp.where(negative, jax.nn.sigmoid(score - score[:, 0:1] + MARGIN), 0.0)
    slope_sum = jnp.sum(slope, axis=1, keepdims=True)
    coef = jnp.where(lane32 == 0, -slope_sum, slope)
    along = jnp.sum(coef * score, axis=1, keepdims=True)
    grad_unit = jnp.zeros((G, L), F32)
    for k in range(C):
        grad_unit = grad_unit + spread(coef, k) * cand[k]
    unit = act / norm
    grad_act = (grad_unit - unit * along) / norm
    grad_pre = grad_act * gate * (1.0 + pre * (1.0 - gate))
    gp16 = grad_pre.astype(BF16)
    gp32 = gp16.astype(F32)

    def swap(n, half_of):
        for k in range(NE):
            half_out[n, k] = half_of(1 - c, k // NX, k % NX).reshape(NZ * Q, L).astype(BF16)
        send(half_out.at[n], half_in.at[n], HALF_ + n, partner)

    def scatter(n, half_of):
        done(half_in.at[n], HALF_ + n).wait_recv()
        for k in range(NE):
            own = half_of(c, k // NX, k % NX).reshape(NZ * Q, L)
            face_out[n, k] = (own + half_in[n, k].astype(F32)).astype(BF16)
        each(NE, lambda i: send(
            face_out.at[n, on_face(i)[0]], face_in.at[n, e], FACE_ + n, on_face(i)[1]))
        face_in[n, e] = face_out[n, e]

    def half_x(core, yy, xx):
        return rx[core, :, yy, xx]

    def half_w(core, yy, xx):
        return rw[:, yy, core, xx]

    def half_y(core, yy, xx):
        return ry[core, :, yy, xx]

    rx[...] = tdot(hot[0], (gp32 * inv).astype(BF16)).reshape(2, NZ, NY, NX, Q, L)
    swap(0, half_x)

    for m in range((C + 1) // 2):
        k = 2 * m
        last = zero if k + 1 == C else hit(ids_lo, K + k + 1, spread(coef, k + 1))
        cand_lo[:, k * Q:(k + 2) * Q] = pair(hit(ids_lo, K + k, spread(coef, k)), last)
    outer(w2, cand_hi, cand_lo)
    ry[...] = tdot(w2[...], unit.astype(BF16)).reshape(2, NZ, NY, NX, Q, L)
    swap(1, half_y)
    scatter(0, half_x)

    done(sf_all.at[pl.ds(0, NZ - 1)], SF_).wait_recv()
    self2 = sf_all[...].reshape(2 * G, 512)
    blank = jnp.zeros((Q, L), F32)
    pieces = []
    for j in range(NZ):
        part = gp32[j * Q:(j + 1) * Q]
        pieces.append(jnp.concatenate([part, blank], axis=1))
        pieces.append(jnp.concatenate([blank, part], axis=1))
    gp2 = jnp.concatenate(pieces, axis=0).astype(BF16)
    gw_self = tdot(self2, gp2)
    rw[0:2] = gw_self[:, :L].reshape(2, NY, 2, NX, Q, L)
    rw[2:4] = gw_self[:, L:].reshape(2, NY, 2, NX, Q, L)
    rw[4:8] = tdot(pool_all, gp16).reshape(4, NY, 2, NX, Q, L)
    swap(2, half_w)
    scatter(1, half_y)

    gsend[...] = gp32.reshape(NZ, Q, L)
    each(NZ, lambda i: send(gsend.at[on_line(i)[0]], grecv.at[z], GP_, on_line(i)[1]))
    grecv[z] = gsend[z]
    scatter(2, half_w)

    done(grecv.at[pl.ds(0, NZ - 1)], GP_).wait_recv()
    gp_own = jnp.concatenate([grecv[f] for f in range(NZ)], axis=1).astype(BF16)
    o_self[...] = ntdot(gp_own, wtop[...])

    def finish(n):
        done(face_in.at[n, pl.ds(0, NE - 1)], FACE_ + n).wait_recv()
        acc = face_in[n, 0].astype(F32)
        for k in range(1, NE):
            acc = acc + face_in[n, k].astype(F32)
        line_out[n] = acc.reshape(NZ, Q, L)
        line_in[n, z] = line_out[n, z]
        each(NZ, lambda i: send(
            line_out.at[n, on_line(i)[0]], line_in.at[n, z], LINE_ + n, on_line(i)[1]))

    def row_sums(n):
        done(line_in.at[n, pl.ds(0, NZ - 1)], LINE_ + n).wait_recv()
        return jnp.concatenate([line_in[n, f] for f in range(NZ)], axis=1)

    finish(0)
    finish(1)
    finish(2)
    before = row_sums(0)
    rest = before - before.astype(BF16).astype(F32)
    loads[2].wait()
    after = ntdot(jnp.concatenate([before, rest], axis=0).astype(BF16), wbot[...])
    o_t[...] = after[0:Q] + after[Q:2 * Q] + row_sums(1)
    o_w[...] = row_sums(2)

    for ref, row in (
        (qi.at[pl.ds(0, NZ - 1)], QI_), (sf_all.at[pl.ds(0, NZ - 1)], SF_),
        (t_all.at[c], TP_), (pooled.at[pl.ds(0, NZ - 1)], PO_),
        (parts.at[pl.ds(0, NZ - 1)], PC_), (gsend.at[pl.ds(0, NZ - 1)], GP_),
        (ps_out.at[pl.ds(0, NZ - 1)], PS_),
    ):
        done(ref, row).wait_send()
    for k in range(NZ):
        if k:
            done(t_all.at[c, b], TZ_ + k).wait_send()
        done(t_all.at[c, pl.ds(0, NY - 1)], TY_ + k).wait_send()
    for n in range(3):
        done(half_out.at[n], HALF_ + n).wait_send()
        done(face_out.at[n, pl.ds(0, NE - 1)], FACE_ + n).wait_send()
        done(line_out.at[n, pl.ds(0, NZ - 1)], LINE_ + n).wait_send()


def hand_over(a, b, c, to_a, to_b, to_c):
    to_a[...] = a[...]
    to_b[...] = b[...]
    to_c[...] = c[...]


def local(table, self_feat, weight, owners, item_rows, importance):
    vmem = pl.BlockSpec(memory_space=pltpu.VMEM)
    hbm = pl.BlockSpec(memory_space=pl.ANY)
    out = jax.ShapeDtypeStruct((Q, 1024), F32)
    V = pltpu.VMEM
    grads = pl.pallas_call(
        kernel,
        out_shape=(out, out, out),
        in_specs=[hbm] * 6,
        out_specs=(vmem, vmem, vmem),
        scratch_shapes=[
            V((32, 1024), BF16),
            V((Q, 1024), BF16),
            V((Q, K + C), jnp.int32),
            V((Q, K + C), jnp.int32),
            V((Q, K), jnp.int32),
            V((2, NB, 32, L), BF16),
            V((NZ, Q, L), jnp.int32),
            V((NZ, 2 * Q, 512), BF16),
            V((NZ, Q, L), F32),
            V((NZ, Q, L), F32),
            V((NZ, G, L), BF16),
            V((NZ, 2 * Q, L), F32),
            V((NZ, Q, L), F32),
            V((NZ, Q, L), F32),
            V((1 + C, G, ITEMS), BF16),
            V((C, G, L), jnp.int32),
            V((C, G, L), F32),
            V((G, ITEMS), BF16),
            V((NZ, K * Q, L), BF16),
            V((NZ, K * Q, L), BF16),
            V((NZ, (C + 1) * Q, L), BF16),
            V((NZ, (C + 1) * Q, L), BF16),
            V((1024, L), BF16),
            V((1024, 1024), BF16),
            V((1024, 1024), BF16),
            V((2, NZ, NY, NX, Q, L), F32),
            V((NZ, NY, 2, NX, Q, L), F32),
            V((2, NZ, NY, NX, Q, L), F32),
            V((3, NE, G, L), BF16),
            V((3, NE, G, L), BF16),
            V((3, NE, G, L), BF16),
            V((3, NE, G, L), BF16),
            V((3, NZ, Q, L), F32),
            V((3, NZ, Q, L), F32),
            pltpu.SemaphoreType.DMA((32, 2)),
            pltpu.SemaphoreType.DMA((8,)),
        ],
        compiler_params=pltpu.CompilerParams(
            collective_id=0, has_side_effects=True, vmem_limit_bytes=62 * 1024 * 1024
        ),
    )(table, self_feat, owners.reshape(Q, K + C), item_rows, importance, weight)
    return pl.pallas_call(
        hand_over, out_shape=(out, out, out), in_specs=[vmem] * 3, out_specs=(vmem,) * 3
    )(*grads)


def solution(mesh):
    both = ("shard", "rep")
    in_specs = (
        P("shard", None), P(both, None), P(), P(both, None, None), P(both, None), P(both, None),
    )
    out_specs = (P(both, None), P(both, None), P(both, None))
    return jax.shard_map(local, mesh=mesh, in_specs=in_specs, out_specs=out_specs, check_vma=False)
```

time: 63.5 us -> 53.2 us (0.84)
  local copies, waits for them, and re-layouts: 5.59 us -> 0 us
  Pallas kernels: 55.6 us -> 52.4 us
  other arithmetic: 1.41 us -> 0 us
    unnamed x9 -> x0, local copies, waits for them, and re-layouts: 5.59 us -> none
    pallas_call x1 -> x2, Pallas kernels: 55.6 us -> 52.4 us  [the longest x1 50.9 us: local(): pl.pallas_call(kernel, out_shape=(out, out, out), in_specs=[hbm] * 6, out...]
    add x1 -> x0, other arithmetic: 0.72 us -> none  [local(): at = own % 2 * HALF + own // 2 * 32 + item_rows]
    concatenate x1 -> x0, other arithmetic: 0.69 us -> none  [local(): jnp.concatenate([jnp.pad(at, ((0, 0), (0, L - K - C))), jnp.pad(importanc...]
where the time goes in v2:
time: 53.2 us; the launch traced here: 53 us
  Pallas kernels  52.4 us (98%)
  between operations  0.64 us (1%)
    pallas_call x1, Pallas kernels, local(): pl.pallas_call(kernel, out_shape=(out, out, out), in_specs=[hbm] * 6, out...  50.9 us
    pallas_call x1, Pallas kernels, local(): pl.pallas_call(hand_over, out_shape=(out, out, out), in_specs=[vmem] * 3,...  1.43 us

profile of v2, /device:TPU:1, one launch (start us, length us, event | category | flops | bytes accessed | tf_op | source)
XLA Modules:
  0.0 53.0 jit_solution(9433167117412772002)
XLA Ops:
  0.6 50.9 %shard_map.85 = (f32[8,1024]{1,0:T(8,128)}, f32[8,1024]{1,0:T(8,128)}, f32[8,1024]{1,0:T(8,128)}) custom-call(bf16[32,1024]{1,0:T(8,128)(2,1)} %tab_hbm.1, bf16[8,1024]{1,0:T(8,128)(2,1)} %sf_hbm.1, s32[8,67]{1,0:T(8,128)} %bitcast.1, s32[8,67]{1,0:T(8,128)} %row_hbm.1, s32[8,50]{1,0:T(8,128)} %imp_hbm.1, bf16[2048,1024]{1,0:T(8,128)(2,1)} %w_hbm.1), custom_call_target="tpu_custom_call" | custom-call | tf_op jit(solution)/shard_map/pallas_call | solution.py:356
  51.6 1.4 %shard_map.86 = (f32[8,1024]{1,0:T(8,128)}, f32[8,1024]{1,0:T(8,128)}, f32[8,1024]{1,0:T(8,128)}) custom-call(f32[8,1024]{1,0:T(8,128)} %get-tuple-element.6.a, f32[8,1024]{1,0:T(8,128)} %get-tuple-element.7.b, f32[8,1024]{1,0:T(8,128)} %get-tuple-element.8.c), custom_call_target="tpu_custom_call" | custom-call | tf_op jit(solution)/shard_map/pallas_call | solution.py:403

commit v3 on v2

--- a/solution.py
+++ b/solution.py
@@ -19,9 +19,9 @@
 ITEMS = 2048
 HALF = ITEMS // 2
 F32, BF16 = jnp.float32, jnp.bfloat16
-QI_, SF_, TP_, PO_, PC_, GP_, PS_ = range(7)
-HALF_, FACE_, LINE_ = 7, 10, 13
-TZ_, TY_ = 16, 24
+QI_, SF_, TP_, PO_, PC_, GP_, PS_, HP_, GX_ = range(9)
+HALF_, FACE_, LINE_ = 9, 12, 15
+TZ_, TY_ = 18, 26
 
 
 def tdot(a, b):
@@ -35,7 +35,7 @@
 def kernel(
     tab_hbm, sf_hbm, own_hbm, row_hbm, imp_hbm, w_hbm, o_self, o_w, o_t,
     tab, sf, own_in, row_in, imp_in,
-    t_all, qi, sf_all, ps_out, ps_in, pooled, parts, gsend, grecv, hot, id_b, cand, w2,
+    t_all, qi, sf_all, ps_out, ps_in, pooled, parts, gsend, grecv, hot, id_b, cand, w2, hot_in, gx_out, gx_in,
     at_hi, at_lo, cand_hi, cand_lo,
     wf, wtop, wbot, rx, rw, ry, half_out, half_in, face_out, face_in, line_out, line_in,
     sems, wsem,
@@ -97,41 +97,44 @@
     each(NZ, lambda i: greet(on_line(i)[1]))
     each(NE, lambda i: greet(on_face(i)[1]))
     greet(partner)
-    for load in small:
+    small[3].wait()
+    t_all[c, b] = tab[:, zcol]
+    pl.semaphore_wait(bar, NZ - 1 + NE - 1 + 1)
+
+    for k in (4, 3, 5, 2, 6, 1, 7):
+        to_z = (z - k) & (NZ - 1)
+        cols = pl.ds(pl.multiple_of(to_z * L, L), L)
+        send(tab.at[:, cols], t_all.at[c, b], TZ_ + k, ((to_z * NY + y) * 2 + c, x))
+
+    def pass_on(k):
+        at = t_all.at[c, ((z + k) & (NZ - 1)) * NY + y]
+        for dy in range(1, NY):
+            send(at, at, TY_ + k, ((z * NY + ((y + dy) & (NY - 1))) * 2 + c, x))
+        send(at, at, TP_, partner)
+
+    pass_on(0)
+    for load in small[:3]:
         load.wait()
     own = own_in[...]
     at = (own & 1) * HALF + (own >> 1) * 32 + row_in[...]
     qi[z] = jnp.zeros((Q, L), jnp.int32)
     qi[z, :, 0:K + C] = at
     qi[z, :, K + C:2 * K + C] = imp_in[...]
-    own_self = sf[...].astype(F32)
-    sf_all[z] = jnp.concatenate([own_self[:, :512], own_self[:, 512:]], axis=0).astype(BF16)
-    t_all[c, b] = tab[:, zcol]
-    pl.semaphore_wait(bar, NZ - 1 + NE - 1 + 1)
-
     each(NZ, lambda i: send(qi.at[z], qi.at[z], QI_, on_line(i)[1]))
-
-    for k in (4, 3, 5, 2, 6, 1, 7):
-        to_z = (z - k) & (NZ - 1)
-        cols = pl.ds(pl.multiple_of(to_z * L, L), L)
-        send(tab.at[:, cols], t_all.at[c, b], TZ_ + k, ((to_z * NY + y) * 2 + c, x))
-
-    def pass_on(k):
-        at = t_all.at[c, ((z + k) & (NZ - 1)) * NY + y]
-        for dy in range(1, NY):
-            send(at, at, TY_ + k, ((z * NY + ((y + dy) & (NY - 1))) * 2 + c, x))
-        send(at, at, TP_, partner)
-
-    pass_on(0)
+    for k in (1, 7, 2, 6, 3, 5, 4):
+        done(t_all.at[c, b], TZ_ + k).wait_recv()
+        pass_on(k)
+
+    small[4].wait()
     loads[1].wait()
     own_pre = jnp.dot(sf[...], wtop[...], preferred_element_type=F32)
     for f in range(NZ):
         ps_out[f] = own_pre[:, f * L:(f + 1) * L]
     each(NZ, lambda i: send(ps_out.at[on_line(i)[0]], ps_in.at[z], PS_, on_line(i)[1]))
     ps_in[z] = ps_out[z]
-    for k in (1, 7, 2, 6, 3, 5, 4):
-        done(t_all.at[c, b], TZ_ + k).wait_recv()
-        pass_on(k)
+    own_self = sf[...].astype(F32)
+    sf_all[z] = jnp.concatenate([own_self[:, :512], own_self[:, 512:]], axis=0).astype(BF16)
+    each(NZ, lambda i: send(sf_all.at[z], sf_all.at[z], SF_, on_line(i)[1]))
 
     done(qi.at[pl.ds(0, NZ - 1)], QI_).wait_recv()
     ids = qi[...].reshape(G, L)
@@ -180,6 +183,9 @@
     mine = jnp.dot(hot[0], rows, preferred_element_type=F32) * inv
     pooled[z] = mine.astype(BF16)
     each(NZ, lambda i: send(pooled.at[z], pooled.at[z], PO_, on_line(i)[1]))
+    half = pl.ds(pl.multiple_of(c * HALF, HALF), HALF)
+    other = pl.ds(pl.multiple_of((1 - c) * HALF, HALF), HALF)
+    send(hot.at[0, :, other], hot_in, HP_, partner)
     for k in range(C):
         id_b[k] = spread(ids, K + k)
 
@@ -215,7 +221,6 @@
     acc = acc.reshape(2, 4, Q, L)
     parts[z] = (acc[:, 0] + acc[:, 1] + acc[:, 2] + acc[:, 3]).reshape(2 * Q, L)
     each(NZ, lambda i: send(parts.at[z], parts.at[z], PC_, on_line(i)[1]))
-    each(NZ, lambda i: send(sf_all.at[z], sf_all.at[z], SF_, on_line(i)[1]))
     done(parts.at[pl.ds(0, NZ - 1)], PC_).wait_recv()
     total = parts[0]
     for f in range(1, NZ):
@@ -251,21 +256,21 @@
         for k in range(NE):
             own = half_of(c, k // NX, k % NX).reshape(NZ * Q, L)
             face_out[n, k] = (own + half_in[n, k].astype(F32)).astype(BF16)
+        spread_out(n)
+
+    def spread_out(n):
         each(NE, lambda i: send(
             face_out.at[n, on_face(i)[0]], face_in.at[n, e], FACE_ + n, on_face(i)[1]))
         face_in[n, e] = face_out[n, e]
 
-    def half_x(core, yy, xx):
-        return rx[core, :, yy, xx]
-
     def half_w(core, yy, xx):
         return rw[:, yy, core, xx]
 
     def half_y(core, yy, xx):
         return ry[core, :, yy, xx]
 
-    rx[...] = tdot(hot[0], (gp32 * inv).astype(BF16)).reshape(2, NZ, NY, NX, Q, L)
-    swap(0, half_x)
+    gx_out[...] = (gp32 * inv).astype(BF16)
+    send(gx_out, gx_in, GX_, partner)
 
     for m in range((C + 1) // 2):
         k = 2 * m
@@ -274,7 +279,13 @@
     outer(w2, cand_hi, cand_lo)
     ry[...] = tdot(w2[...], unit.astype(BF16)).reshape(2, NZ, NY, NX, Q, L)
     swap(1, half_y)
-    scatter(0, half_x)
+    done(hot_in, HP_).wait_recv()
+    mine_x = tdot(hot[0, :, half], gx_out[...])
+    done(gx_in, GX_).wait_recv()
+    rx[...] = (mine_x + tdot(hot_in[...], gx_in[...])).reshape(NZ, NY, NX, Q, L)
+    for k in range(NE):
+        face_out[0, k] = rx[:, k // NX, k % NX].reshape(NZ * Q, L).astype(BF16)
+    spread_out(0)
 
     done(sf_all.at[pl.ds(0, NZ - 1)], SF_).wait_recv()
     self2 = sf_all[...].reshape(2 * G, 512)
@@ -329,7 +340,7 @@
         (qi.at[pl.ds(0, NZ - 1)], QI_), (sf_all.at[pl.ds(0, NZ - 1)], SF_),
         (t_all.at[c], TP_), (pooled.at[pl.ds(0, NZ - 1)], PO_),
         (parts.at[pl.ds(0, NZ - 1)], PC_), (gsend.at[pl.ds(0, NZ - 1)], GP_),
-        (ps_out.at[pl.ds(0, NZ - 1)], PS_),
+        (ps_out.at[pl.ds(0, NZ - 1)], PS_), (hot.at[0, :, other], HP_), (gx_out, GX_),
     ):
         done(ref, row).wait_send()
     for k in range(NZ):
@@ -337,7 +348,8 @@
             done(t_all.at[c, b], TZ_ + k).wait_send()
         done(t_all.at[c, pl.ds(0, NY - 1)], TY_ + k).wait_send()
     for n in range(3):
-        done(half_out.at[n], HALF_ + n).wait_send()
+        if n:
+            done(half_out.at[n], HALF_ + n).wait_send()
         done(face_out.at[n, pl.ds(0, NE - 1)], FACE_ + n).wait_send()
         done(line_out.at[n, pl.ds(0, NZ - 1)], LINE_ + n).wait_send()
 
@@ -377,6 +389,9 @@
             V((C, G, L), jnp.int32),
             V((C, G, L), F32),
             V((G, ITEMS), BF16),
+            V((G, HALF), BF16),
+            V((G, L), BF16),
+            V((G, L), BF16),
             V((NZ, K * Q, L), BF16),
             V((NZ, K * Q, L), BF16),
             V((NZ, (C + 1) * Q, L), BF16),
@@ -384,7 +399,7 @@
             V((1024, L), BF16),
             V((1024, 1024), BF16),
             V((1024, 1024), BF16),
-            V((2, NZ, NY, NX, Q, L), F32),
+            V((NZ, NY, NX, Q, L), F32),
             V((NZ, NY, 2, NX, Q, L), F32),
             V((2, NZ, NY, NX, Q, L), F32),
             V((3, NE, G, L), BF16),
@@ -393,7 +408,7 @@
             V((3, NE, G, L), BF16),
             V((3, NZ, Q, L), F32),
             V((3, NZ, Q, L), F32),
-            pltpu.SemaphoreType.DMA((32, 2)),
+            pltpu.SemaphoreType.DMA((34, 2)),
             pltpu.SemaphoreType.DMA((8,)),
         ],
         compiler_params=pltpu.CompilerParams(

time: 53.2 us -> 51.7 us (0.972)
  Pallas kernels: 52.4 us -> 50.9 us
    pallas_call x1, Pallas kernels: 50.9 us -> 49.5 us  [local(): pl.pallas_call(kernel, out_shape=(out, out, out), in_specs=[hbm] * 6, out...]
where the time goes in v3:
time: 51.7 us; the launch traced here: 51.5 us
  Pallas kernels  50.9 us (98%)
  between operations  0.64 us (1%)
    pallas_call x1, Pallas kernels, local(): pl.pallas_call(kernel, out_shape=(out, out, out), in_specs=[hbm] * 6, out...  49.5 us
    pallas_call x1, Pallas kernels, local(): pl.pallas_call(hand_over, out_shape=(out, out, out), in_specs=[vmem] * 3,...  1.43 us

profile of v3, /device:TPU:1, one launch (start us, length us, event | category | flops | bytes accessed | tf_op | source)
XLA Modules:
  0.0 51.5 jit_solution(6678040349250498157)
XLA Ops:
  0.6 49.5 %shard_map.85 = (f32[8,1024]{1,0:T(8,128)}, f32[8,1024]{1,0:T(8,128)}, f32[8,1024]{1,0:T(8,128)}) custom-call(bf16[32,1024]{1,0:T(8,128)(2,1)} %tab_hbm.1, bf16[8,1024]{1,0:T(8,128)(2,1)} %sf_hbm.1, s32[8,67]{1,0:T(8,128)} %bitcast.1, s32[8,67]{1,0:T(8,128)} %row_hbm.1, s32[8,50]{1,0:T(8,128)} %imp_hbm.1, bf16[2048,1024]{1,0:T(8,128)(2,1)} %w_hbm.1), custom_call_target="tpu_custom_call" | custom-call | tf_op jit(solution)/shard_map/pallas_call | solution.py:368
  50.1 1.4 %shard_map.86 = (f32[8,1024]{1,0:T(8,128)}, f32[8,1024]{1,0:T(8,128)}, f32[8,1024]{1,0:T(8,128)}) custom-call(f32[8,1024]{1,0:T(8,128)} %get-tuple-element.6.a, f32[8,1024]{1,0:T(8,128)} %get-tuple-element.7.b, f32[8,1024]{1,0:T(8,128)} %get-tuple-element.8.c), custom_call_target="tpu_custom_call" | custom-call | tf_op jit(solution)/shard_map/pallas_call | solution.py:418

commit v4 on v3

--- a/solution.py
+++ b/solution.py
@@ -20,8 +20,8 @@
 HALF = ITEMS // 2
 F32, BF16 = jnp.float32, jnp.bfloat16
 QI_, SF_, TP_, PO_, PC_, GP_, PS_, HP_, GX_ = range(9)
-HALF_, FACE_, LINE_ = 9, 12, 15
-TZ_, TY_ = 18, 26
+HALF_, LINE_, FACE_ = 9, 12, 15
+TZ_, TY_ = 21, 29
 
 
 def tdot(a, b):
@@ -256,12 +256,15 @@
         for k in range(NE):
             own = half_of(c, k // NX, k % NX).reshape(NZ * Q, L)
             face_out[n, k] = (own + half_in[n, k].astype(F32)).astype(BF16)
-        spread_out(n)
-
-    def spread_out(n):
+        face_in[n, e] = face_out[n, e]
+
+    PART = NZ // 2 * Q
+
+    def spread_out(n, part):
+        rows_at = pl.ds(part * PART, PART)
         each(NE, lambda i: send(
-            face_out.at[n, on_face(i)[0]], face_in.at[n, e], FACE_ + n, on_face(i)[1]))
-        face_in[n, e] = face_out[n, e]
+            face_out.at[n, on_face(i)[0], rows_at], face_in.at[n, e, rows_at],
+            FACE_ + 2 * n + part, on_face(i)[1]))
 
     def half_w(core, yy, xx):
         return rw[:, yy, core, xx]
@@ -285,7 +288,8 @@
     rx[...] = (mine_x + tdot(hot_in[...], gx_in[...])).reshape(NZ, NY, NX, Q, L)
     for k in range(NE):
         face_out[0, k] = rx[:, k // NX, k % NX].reshape(NZ * Q, L).astype(BF16)
-    spread_out(0)
+    face_in[0, e] = face_out[0, e]
+    spread_out(0, 0)
 
     done(sf_all.at[pl.ds(0, NZ - 1)], SF_).wait_recv()
     self2 = sf_all[...].reshape(2 * G, 512)
@@ -302,33 +306,45 @@
     rw[4:8] = tdot(pool_all, gp16).reshape(4, NY, 2, NX, Q, L)
     swap(2, half_w)
     scatter(1, half_y)
+    spread_out(1, 0)
+    spread_out(0, 1)
 
     gsend[...] = gp32.reshape(NZ, Q, L)
     each(NZ, lambda i: send(gsend.at[on_line(i)[0]], grecv.at[z], GP_, on_line(i)[1]))
     grecv[z] = gsend[z]
     scatter(2, half_w)
+    spread_out(2, 0)
+    spread_out(1, 1)
+    spread_out(2, 1)
 
     done(grecv.at[pl.ds(0, NZ - 1)], GP_).wait_recv()
     gp_own = jnp.concatenate([grecv[f] for f in range(NZ)], axis=1).astype(BF16)
     o_self[...] = ntdot(gp_own, wtop[...])
 
-    def finish(n):
-        done(face_in.at[n, pl.ds(0, NE - 1)], FACE_ + n).wait_recv()
-        acc = face_in[n, 0].astype(F32)
+    def finish(n, part):
+        rows_at = pl.ds(part * PART, PART)
+        done(face_in.at[n, pl.ds(0, NE - 1), rows_at], FACE_ + 2 * n + part).wait_recv()
+        acc = face_in[n, 0, rows_at].astype(F32)
         for k in range(1, NE):
-            acc = acc + face_in[n, k].astype(F32)
-        line_out[n] = acc.reshape(NZ, Q, L)
-        line_in[n, z] = line_out[n, z]
-        each(NZ, lambda i: send(
-            line_out.at[n, on_line(i)[0]], line_in.at[n, z], LINE_ + n, on_line(i)[1]))
+            acc = acc + face_in[n, k, rows_at].astype(F32)
+        first = part * (NZ // 2)
+        line_out[n, first:first + NZ // 2] = acc.reshape(NZ // 2, Q, L)
+        for to_z in range(first, first + NZ // 2):
+            @pl.when(z == to_z)
+            def _():
+                line_in[n, to_z] = line_out[n, to_z]
+
+            @pl.when(z != to_z)
+            def _():
+                send(line_out.at[n, to_z], line_in.at[n, z], LINE_ + n, ((to_z * NY + y) * 2 + c, x))
 
     def row_sums(n):
         done(line_in.at[n, pl.ds(0, NZ - 1)], LINE_ + n).wait_recv()
         return jnp.concatenate([line_in[n, f] for f in range(NZ)], axis=1)
 
-    finish(0)
-    finish(1)
-    finish(2)
+    for part in range(2):
+        for n in range(3):
+            finish(n, part)
     before = row_sums(0)
     rest = before - before.astype(BF16).astype(F32)
     loads[2].wait()
@@ -350,7 +366,9 @@
     for n in range(3):
         if n:
             done(half_out.at[n], HALF_ + n).wait_send()
-        done(face_out.at[n, pl.ds(0, NE - 1)], FACE_ + n).wait_send()
+        for part in range(2):
+            rows_at = pl.ds(part * PART, PART)
+            done(face_out.at[n, pl.ds(0, NE - 1), rows_at], FACE_ + 2 * n + part).wait_send()
         done(line_out.at[n, pl.ds(0, NZ - 1)], LINE_ + n).wait_send()
 
 
@@ -408,7 +426,7 @@
             V((3, NE, G, L), BF16),
             V((3, NZ, Q, L), F32),
             V((3, NZ, Q, L), F32),
-            pltpu.SemaphoreType.DMA((34, 2)),
+            pltpu.SemaphoreType.DMA((37, 2)),
             pltpu.SemaphoreType.DMA((8,)),
         ],
         compiler_params=pltpu.CompilerParams(

time: 51.7 us -> 49.2 us (0.952)
  Pallas kernels: 50.9 us -> 48.4 us
    pallas_call x1, Pallas kernels: 49.5 us -> 47 us  [local(): pl.pallas_call(kernel, out_shape=(out, out, out), in_specs=[hbm] * 6, out...]
where the time goes in v4:
time: 49.2 us; the launch traced here: 49.1 us
  Pallas kernels  48.4 us (98%)
  between operations  0.64 us (1%)
    pallas_call x1, Pallas kernels, local(): pl.pallas_call(kernel, out_shape=(out, out, out), in_specs=[hbm] * 6, out...  47 us
    pallas_call x1, Pallas kernels, local(): pl.pallas_call(hand_over, out_shape=(out, out, out), in_specs=[vmem] * 3,...  1.43 us

profile of v4, /device:TPU:1, one launch (start us, length us, event | category | flops | bytes accessed | tf_op | source)
XLA Modules:
  0.0 49.1 jit_solution(15193138193683298971)
XLA Ops:
  0.6 47.0 %shard_map.85 = (f32[8,1024]{1,0:T(8,128)}, f32[8,1024]{1,0:T(8,128)}, f32[8,1024]{1,0:T(8,128)}) custom-call(bf16[32,1024]{1,0:T(8,128)(2,1)} %tab_hbm.1, bf16[8,1024]{1,0:T(8,128)(2,1)} %sf_hbm.1, s32[8,67]{1,0:T(8,128)} %bitcast.1, s32[8,67]{1,0:T(8,128)} %row_hbm.1, s32[8,50]{1,0:T(8,128)} %imp_hbm.1, bf16[2048,1024]{1,0:T(8,128)(2,1)} %w_hbm.1), custom_call_target="tpu_custom_call" | custom-call | tf_op jit(solution)/shard_map/pallas_call | solution.py:386
  47.6 1.4 %shard_map.86 = (f32[8,1024]{1,0:T(8,128)}, f32[8,1024]{1,0:T(8,128)}, f32[8,1024]{1,0:T(8,128)}) custom-call(f32[8,1024]{1,0:T(8,128)} %get-tuple-element.6.a, f32[8,1024]{1,0:T(8,128)} %get-tuple-element.7.b, f32[8,1024]{1,0:T(8,128)} %get-tuple-element.8.c), custom_call_target="tpu_custom_call" | custom-call | tf_op jit(solution)/shard_map/pallas_call | solution.py:436

commit v5 on v4

--- a/solution.py
+++ b/solution.py
@@ -49,13 +49,16 @@
     e = y * NX + x
     partner = (b * 2 + 1 - c, x)
 
-    def on_line(off):
-        other = (z + off) & (NZ - 1)
-        return other, ((other * NY + y) * 2 + c, x)
-
-    def on_face(off):
-        other = (e + off) & (NE - 1)
-        return other, ((z * NY + (other >> 2)) * 2 + c, (other & (NX - 1)))
+    def on_line():
+        for k in (4, 3, 5, 2, 6, 1, 7):
+            other = (z + k) & (NZ - 1)
+            yield other, ((other * NY + y) * 2 + c, x)
+
+    def on_face():
+        steps = [(dy, dx) for dy in range(NY) for dx in range(NX)][1:]
+        for dy, dx in sorted(steps, key=lambda step: -min(step[0], 4 - step[0]) - min(step[1], 4 - step[1])):
+            yy, xx = (y + dy) & (NY - 1), (x + dx) & (NX - 1)
+            yield yy * NX + xx, ((z * NY + yy) * 2 + c, xx)
 
     def send(src, dst, row, to):
         pltpu.make_async_remote_copy(
@@ -68,12 +71,6 @@
             src_ref=ref, dst_ref=ref, send_sem=sems.at[row, 0], recv_sem=sems.at[row, 1],
             device_id=partner, device_id_type=MESH,
         )
-
-    def each(n, body):
-        def step(i, carry):
-            body(i)
-            return carry
-        lax.fori_loop(1, n, step, 0)
 
     zcol = pl.ds(pl.multiple_of(z * L, L), L)
     loads = [
@@ -94,8 +91,8 @@
     def greet(to):
         pl.semaphore_signal(bar, inc=1, device_id=to, device_id_type=MESH)
 
-    each(NZ, lambda i: greet(on_line(i)[1]))
-    each(NE, lambda i: greet(on_face(i)[1]))
+    for _, to in [*on_line(), *on_face()]:
+        greet(to)
     greet(partner)
     small[3].wait()
     t_all[c, b] = tab[:, zcol]
@@ -120,7 +117,8 @@
     qi[z] = jnp.zeros((Q, L), jnp.int32)
     qi[z, :, 0:K + C] = at
     qi[z, :, K + C:2 * K + C] = imp_in[...]
-    each(NZ, lambda i: send(qi.at[z], qi.at[z], QI_, on_line(i)[1]))
+    for _, to in on_line():
+        send(qi.at[z], qi.at[z], QI_, to)
     for k in (1, 7, 2, 6, 3, 5, 4):
         done(t_all.at[c, b], TZ_ + k).wait_recv()
         pass_on(k)
@@ -130,11 +128,13 @@
     own_pre = jnp.dot(sf[...], wtop[...], preferred_element_type=F32)
     for f in range(NZ):
         ps_out[f] = own_pre[:, f * L:(f + 1) * L]
-    each(NZ, lambda i: send(ps_out.at[on_line(i)[0]], ps_in.at[z], PS_, on_line(i)[1]))
+    for other, to in on_line():
+        send(ps_out.at[other], ps_in.at[z], PS_, to)
     ps_in[z] = ps_out[z]
     own_self = sf[...].astype(F32)
     sf_all[z] = jnp.concatenate([own_self[:, :512], own_self[:, 512:]], axis=0).astype(BF16)
-    each(NZ, lambda i: send(sf_all.at[z], sf_all.at[z], SF_, on_line(i)[1]))
+    for _, to in on_line():
+        send(sf_all.at[z], sf_all.at[z], SF_, to)
 
     done(qi.at[pl.ds(0, NZ - 1)], QI_).wait_recv()
     ids = qi[...].reshape(G, L)
@@ -182,10 +182,11 @@
     rows = t_all[...].reshape(ITEMS, L)
     mine = jnp.dot(hot[0], rows, preferred_element_type=F32) * inv
     pooled[z] = mine.astype(BF16)
-    each(NZ, lambda i: send(pooled.at[z], pooled.at[z], PO_, on_line(i)[1]))
+    for _, to in on_line():
+        send(pooled.at[z], pooled.at[z], PO_, to)
     half = pl.ds(pl.multiple_of(c * HALF, HALF), HALF)
-    other = pl.ds(pl.multiple_of((1 - c) * HALF, HALF), HALF)
-    send(hot.at[0, :, other], hot_in, HP_, partner)
+    away = pl.ds(pl.multiple_of((1 - c) * HALF, HALF), HALF)
+    send(hot.at[0, :, away], hot_in, HP_, partner)
     for k in range(C):
         id_b[k] = spread(ids, K + k)
 
@@ -220,7 +221,8 @@
         acc = jnp.where(where_at == k, jnp.sum(act * cand[k], axis=1, keepdims=True), acc)
     acc = acc.reshape(2, 4, Q, L)
     parts[z] = (acc[:, 0] + acc[:, 1] + acc[:, 2] + acc[:, 3]).reshape(2 * Q, L)
-    each(NZ, lambda i: send(parts.at[z], parts.at[z], PC_, on_line(i)[1]))
+    for _, to in on_line():
+        send(parts.at[z], parts.at[z], PC_, to)
     done(parts.at[pl.ds(0, NZ - 1)], PC_).wait_recv()
     total = parts[0]
     for f in range(1, NZ):
@@ -262,9 +264,8 @@
 
     def spread_out(n, part):
         rows_at = pl.ds(part * PART, PART)
-        each(NE, lambda i: send(
-            face_out.at[n, on_face(i)[0], rows_at], face_in.at[n, e, rows_at],
-            FACE_ + 2 * n + part, on_face(i)[1]))
+        for other, to in on_face():
+            send(face_out.at[n, other, rows_at], face_in.at[n, e, rows_at], FACE_ + 2 * n + part, to)
 
     def half_w(core, yy, xx):
         return rw[:, yy, core, xx]
@@ -282,15 +283,6 @@
     outer(w2, cand_hi, cand_lo)
     ry[...] = tdot(w2[...], unit.astype(BF16)).reshape(2, NZ, NY, NX, Q, L)
     swap(1, half_y)
-    done(hot_in, HP_).wait_recv()
-    mine_x = tdot(hot[0, :, half], gx_out[...])
-    done(gx_in, GX_).wait_recv()
-    rx[...] = (mine_x + tdot(hot_in[...], gx_in[...])).reshape(NZ, NY, NX, Q, L)
-    for k in range(NE):
-        face_out[0, k] = rx[:, k // NX, k % NX].reshape(NZ * Q, L).astype(BF16)
-    face_in[0, e] = face_out[0, e]
-    spread_out(0, 0)
-
     done(sf_all.at[pl.ds(0, NZ - 1)], SF_).wait_recv()
     self2 = sf_all[...].reshape(2 * G, 512)
     blank = jnp.zeros((Q, L), F32)
@@ -305,15 +297,24 @@
     rw[2:4] = gw_self[:, L:].reshape(2, NY, 2, NX, Q, L)
     rw[4:8] = tdot(pool_all, gp16).reshape(4, NY, 2, NX, Q, L)
     swap(2, half_w)
+    done(hot_in, HP_).wait_recv()
+    mine_x = tdot(hot[0, :, half], gx_out[...])
+    done(gx_in, GX_).wait_recv()
+    rx[...] = (mine_x + tdot(hot_in[...], gx_in[...])).reshape(NZ, NY, NX, Q, L)
+    for k in range(NE):
+        face_out[0, k] = rx[:, k // NX, k % NX].reshape(NZ * Q, L).astype(BF16)
+    face_in[0, e] = face_out[0, e]
+    spread_out(0, 0)
     scatter(1, half_y)
     spread_out(1, 0)
-    spread_out(0, 1)
 
     gsend[...] = gp32.reshape(NZ, Q, L)
-    each(NZ, lambda i: send(gsend.at[on_line(i)[0]], grecv.at[z], GP_, on_line(i)[1]))
+    for other, to in on_line():
+        send(gsend.at[other], grecv.at[z], GP_, to)
     grecv[z] = gsend[z]
     scatter(2, half_w)
     spread_out(2, 0)
+    spread_out(0, 1)
     spread_out(1, 1)
     spread_out(2, 1)
 
@@ -356,7 +357,7 @@
         (qi.at[pl.ds(0, NZ - 1)], QI_), (sf_all.at[pl.ds(0, NZ - 1)], SF_),
         (t_all.at[c], TP_), (pooled.at[pl.ds(0, NZ - 1)], PO_),
         (parts.at[pl.ds(0, NZ - 1)], PC_), (gsend.at[pl.ds(0, NZ - 1)], GP_),
-        (ps_out.at[pl.ds(0, NZ - 1)], PS_), (hot.at[0, :, other], HP_), (gx_out, GX_),
+        (ps_out.at[pl.ds(0, NZ - 1)], PS_), (hot.at[0, :, away], HP_), (gx_out, GX_),
     ):
         done(ref, row).wait_send()
     for k in range(NZ):

time: 49.2 us -> 47.4 us (0.963)
  Pallas kernels: 48.4 us -> 46.6 us
    pallas_call x1, Pallas kernels: 47 us -> 45.1 us  [local(): pl.pallas_call(kernel, out_shape=(out, out, out), in_specs=[hbm] * 6, out...]
where the time goes in v5:
time: 47.4 us; the launch traced here: 47.2 us
  Pallas kernels  46.6 us (98%)
  between operations  0.64 us (1%)
    pallas_call x1, Pallas kernels, local(): pl.pallas_call(kernel, out_shape=(out, out, out), in_specs=[hbm] * 6, out...  45.1 us
    pallas_call x1, Pallas kernels, local(): pl.pallas_call(hand_over, out_shape=(out, out, out), in_specs=[vmem] * 3,...  1.43 us

profile of v5, /device:TPU:1, one launch (start us, length us, event | category | flops | bytes accessed | tf_op | source)
XLA Modules:
  0.0 47.2 jit_solution(317117013161119185)
XLA Ops:
  0.6 45.1 %shard_map.85 = (f32[8,1024]{1,0:T(8,128)}, f32[8,1024]{1,0:T(8,128)}, f32[8,1024]{1,0:T(8,128)}) custom-call(bf16[32,1024]{1,0:T(8,128)(2,1)} %tab_hbm.1, bf16[8,1024]{1,0:T(8,128)(2,1)} %sf_hbm.1, s32[8,67]{1,0:T(8,128)} %bitcast.1, s32[8,67]{1,0:T(8,128)} %row_hbm.1, s32[8,50]{1,0:T(8,128)} %imp_hbm.1, bf16[2048,1024]{1,0:T(8,128)(2,1)} %w_hbm.1), custom_call_target="tpu_custom_call" | custom-call | tf_op jit(solution)/shard_map/pallas_call | solution.py:387
  45.8 1.4 %shard_map.86 = (f32[8,1024]{1,0:T(8,128)}, f32[8,1024]{1,0:T(8,128)}, f32[8,1024]{1,0:T(8,128)}) custom-call(f32[8,1024]{1,0:T(8,128)} %get-tuple-element.6.a, f32[8,1024]{1,0:T(8,128)} %get-tuple-element.7.b, f32[8,1024]{1,0:T(8,128)} %get-tuple-element.8.c), custom_call_target="tpu_custom_call" | custom-call | tf_op jit(solution)/shard_map/pallas_call | solution.py:437

commit v6 on v5

--- a/solution.py
+++ b/solution.py
@@ -19,9 +19,10 @@
 ITEMS = 2048
 HALF = ITEMS // 2
 F32, BF16 = jnp.float32, jnp.bfloat16
-QI_, SF_, TP_, PO_, PC_, GP_, PS_, HP_, GX_ = range(9)
-HALF_, LINE_, FACE_ = 9, 12, 15
-TZ_, TY_ = 21, 29
+PARTS = ((0, 4), (4, 8))
+QI_, SF_, TP_, PO_, PC_, GP_, PS_, HP_, GX_, W2_, PB_, SB_ = range(12)
+LINE_, FACE_ = 12, 15
+TZ_, TY_ = 24, 32
 
 
 def tdot(a, b):
@@ -37,7 +38,7 @@
     tab, sf, own_in, row_in, imp_in,
     t_all, qi, sf_all, ps_out, ps_in, pooled, parts, gsend, grecv, hot, id_b, cand, w2, hot_in, gx_out, gx_in,
     at_hi, at_lo, cand_hi, cand_lo,
-    wf, wtop, wbot, rx, rw, ry, half_out, half_in, face_out, face_in, line_out, line_in,
+    wf, wtop, wbot, rx, rw, ry, pool_in, self_in, w2_in, face_out, face_in, line_out, line_in,
     sems, wsem,
 ):
     s = lax.axis_index("shard")
@@ -105,7 +106,7 @@
 
     def pass_on(k):
         at = t_all.at[c, ((z + k) & (NZ - 1)) * NY + y]
-        for dy in range(1, NY):
+        for dy in (2, 1, 3):
             send(at, at, TY_ + k, ((z * NY + ((y + dy) & (NY - 1))) * 2 + c, x))
         send(at, at, TP_, partner)
 
@@ -201,6 +202,8 @@
     cand[...] = jnp.dot(
         hot[1:1 + C].reshape(C * G, ITEMS), rows, preferred_element_type=F32
     ).reshape(C, G, L)
+    for k in range(1, C):
+        cand[k] = cand[k] - cand[0]
 
     zero = jnp.zeros((G, L), F32)
     for m in range((C + 1) // 2):
@@ -214,123 +217,132 @@
     pre = ps_in[...].reshape(G, L) + jnp.dot(pool_all, wf[...], preferred_element_type=F32)
     gate = jax.nn.sigmoid(pre)
     act = pre * gate
-    place = 32 * lax.rem(lax.div(lax.broadcasted_iota(jnp.int32, (G, L), 0), Q), 4)
-    where_at = lane - place
-    acc = jnp.where(where_at == C, jnp.sum(act * act, axis=1, keepdims=True), 0.0)
-    for k in range(C):
-        acc = jnp.where(where_at == k, jnp.sum(act * cand[k], axis=1, keepdims=True), acc)
-    acc = acc.reshape(2, 4, Q, L)
-    parts[z] = (acc[:, 0] + acc[:, 1] + acc[:, 2] + acc[:, 3]).reshape(2 * Q, L)
+    sent_rows = pl.ds(0, Q + 1)
+    row = lax.broadcasted_iota(jnp.int32, (G, L), 0)
+    where_at = lane - (C - 1) * (row >> 3)
+    acc = zero
+    for k in range(1, C):
+        acc = jnp.where(where_at == k - 1, jnp.sum(act * cand[k], axis=1, keepdims=True), acc)
+    parts[z, 0:Q] = jnp.sum(acc.reshape(NZ, Q, L), axis=0)
+    squares = jnp.sum(act * act, axis=1, keepdims=True)
+    parts[z, Q:Q + 1] = jnp.sum(jnp.where(row == lane, squares, 0.0), axis=0, keepdims=True)
     for _, to in on_line():
-        send(parts.at[z], parts.at[z], PC_, to)
-    done(parts.at[pl.ds(0, NZ - 1)], PC_).wait_recv()
-    total = parts[0]
+        send(parts.at[z, sent_rows], parts.at[z, sent_rows], PC_, to)
+    done(sf_all.at[pl.ds(0, NZ - 1)], SF_).wait_recv()
+    self2 = sf_all[...].reshape(2 * G, 512)
+    send(pooled, pool_in, PB_, partner)
+    send(sf_all, self_in, SB_, partner)
+    done(parts.at[pl.ds(0, NZ - 1), sent_rows], PC_).wait_recv()
+    total, squares = parts[0, 0:Q], parts[0, Q:Q + 1]
     for f in range(1, NZ):
-        total = total + parts[f]
+        total, squares = total + parts[f, 0:Q], squares + parts[f, Q:Q + 1]
     sums = jnp.concatenate(
-        [total[(j // 4) * Q:(j // 4 + 1) * Q, 32 * (j % 4):32 * (j % 4) + 32] for j in range(NZ)],
-        axis=0,
+        [total[:, (C - 1) * j:(C - 1) * (j + 1)] for j in range(NZ)], axis=0
     )
-    norm = jnp.sqrt(sums[:, C:C + 1] + EPS)
-    score = sums / norm
-    lane32 = lax.broadcasted_iota(jnp.int32, (G, 32), 1)
-    negative = (lane32 >= 1) & (lane32 < C)
-    slope = jnp.where(negative, jax.nn.sigmoid(score - score[:, 0:1] + MARGIN), 0.0)
+    squares = jnp.sum(
+        jnp.where(row == lane, jnp.broadcast_to(squares, (G, L)), 0.0), axis=1, keepdims=True
+    )
+    norm = jnp.sqrt(squares + EPS)
+    ahead = sums / norm
+    slope = jax.nn.sigmoid(ahead + MARGIN)
     slope_sum = jnp.sum(slope, axis=1, keepdims=True)
-    coef = jnp.where(lane32 == 0, -slope_sum, slope)
-    along = jnp.sum(coef * score, axis=1, keepdims=True)
+    along = jnp.sum(slope * ahead, axis=1, keepdims=True)
+
+    def coef(k):
+        if k == 0:
+            return jnp.broadcast_to(-slope_sum, (G, L))
+        return spread(slope, k - 1)
+
     grad_unit = jnp.zeros((G, L), F32)
-    for k in range(C):
-        grad_unit = grad_unit + spread(coef, k) * cand[k]
+    for k in range(1, C):
+        grad_unit = grad_unit + coef(k) * cand[k]
     unit = act / norm
     grad_act = (grad_unit - unit * along) / norm
     grad_pre = grad_act * gate * (1.0 + pre * (1.0 - gate))
     gp16 = grad_pre.astype(BF16)
     gp32 = gp16.astype(F32)
 
-    def swap(n, half_of):
+    def rows_of(part):
+        return pl.ds(PARTS[part][0] * Q, (PARTS[part][1] - PARTS[part][0]) * Q)
+
+    def spread_out(n, part):
+        rows_at = rows_of(part)
+        for other, to in on_face():
+            send(face_out.at[n, other, rows_at], face_in.at[n, e, rows_at], FACE_ + 3 * n + part, to)
+
+    def reduce_half(n, half_of):
         for k in range(NE):
-            half_out[n, k] = half_of(1 - c, k // NX, k % NX).reshape(NZ * Q, L).astype(BF16)
-        send(half_out.at[n], half_in.at[n], HALF_ + n, partner)
-
-    def scatter(n, half_of):
-        done(half_in.at[n], HALF_ + n).wait_recv()
-        for k in range(NE):
-            own = half_of(c, k // NX, k % NX).reshape(NZ * Q, L)
-            face_out[n, k] = (own + half_in[n, k].astype(F32)).astype(BF16)
+            face_out[n, k] = half_of(k // NX, k % NX).reshape(NZ * Q, L).astype(BF16)
         face_in[n, e] = face_out[n, e]
-
-    PART = NZ // 2 * Q
-
-    def spread_out(n, part):
-        rows_at = pl.ds(part * PART, PART)
-        for other, to in on_face():
-            send(face_out.at[n, other, rows_at], face_in.at[n, e, rows_at], FACE_ + 2 * n + part, to)
-
-    def half_w(core, yy, xx):
-        return rw[:, yy, core, xx]
-
-    def half_y(core, yy, xx):
-        return ry[core, :, yy, xx]
-
-    gx_out[...] = (gp32 * inv).astype(BF16)
+        spread_out(n, 0)
+
+    def both_cores(mine, theirs):
+        return jnp.concatenate([mine, theirs], axis=0)
+
+    def two_blocks(rows):
+        blank = jnp.zeros((Q, L), F32)
+        pieces = []
+        for j in range(NZ):
+            part = rows[j * Q:(j + 1) * Q].astype(F32)
+            pieces.append(jnp.concatenate([part, blank], axis=1))
+            pieces.append(jnp.concatenate([blank, part], axis=1))
+        return jnp.concatenate(pieces, axis=0).astype(BF16)
+
+    gx_out[0] = (gp32 * inv).astype(BF16)
+    gx_out[1] = gp16
+    gx_out[2] = unit.astype(BF16)
     send(gx_out, gx_in, GX_, partner)
-
     for m in range((C + 1) // 2):
         k = 2 * m
-        last = zero if k + 1 == C else hit(ids_lo, K + k + 1, spread(coef, k + 1))
-        cand_lo[:, k * Q:(k + 2) * Q] = pair(hit(ids_lo, K + k, spread(coef, k)), last)
+        last = zero if k + 1 == C else hit(ids_lo, K + k + 1, coef(k + 1))
+        cand_lo[:, k * Q:(k + 2) * Q] = pair(hit(ids_lo, K + k, coef(k)), last)
     outer(w2, cand_hi, cand_lo)
-    ry[...] = tdot(w2[...], unit.astype(BF16)).reshape(2, NZ, NY, NX, Q, L)
-    swap(1, half_y)
-    done(sf_all.at[pl.ds(0, NZ - 1)], SF_).wait_recv()
-    self2 = sf_all[...].reshape(2 * G, 512)
-    blank = jnp.zeros((Q, L), F32)
-    pieces = []
-    for j in range(NZ):
-        part = gp32[j * Q:(j + 1) * Q]
-        pieces.append(jnp.concatenate([part, blank], axis=1))
-        pieces.append(jnp.concatenate([blank, part], axis=1))
-    gp2 = jnp.concatenate(pieces, axis=0).astype(BF16)
-    gw_self = tdot(self2, gp2)
+    send(w2.at[:, away], w2_in, W2_, partner)
+    done(hot_in, HP_).wait_recv()
+    done(gx_in, GX_).wait_recv()
+
+    rx[...] = tdot(
+        both_cores(hot[0, :, half], hot_in[...]), both_cores(gx_out[0], gx_in[0])
+    ).reshape(NZ, NY, NX, Q, L)
+    reduce_half(0, lambda yy, xx: rx[:, yy, xx])
+
+    done(pool_in, PB_).wait_recv()
+    done(self_in, SB_).wait_recv()
+    self_rows = both_cores(self2, self_in[...].reshape(2 * G, 512))
+    gw_self = tdot(self_rows, both_cores(two_blocks(gp16), two_blocks(gx_in[1])))
     rw[0:2] = gw_self[:, :L].reshape(2, NY, 2, NX, Q, L)
     rw[2:4] = gw_self[:, L:].reshape(2, NY, 2, NX, Q, L)
-    rw[4:8] = tdot(pool_all, gp16).reshape(4, NY, 2, NX, Q, L)
-    swap(2, half_w)
-    done(hot_in, HP_).wait_recv()
-    mine_x = tdot(hot[0, :, half], gx_out[...])
-    done(gx_in, GX_).wait_recv()
-    rx[...] = (mine_x + tdot(hot_in[...], gx_in[...])).reshape(NZ, NY, NX, Q, L)
-    for k in range(NE):
-        face_out[0, k] = rx[:, k // NX, k % NX].reshape(NZ * Q, L).astype(BF16)
-    face_in[0, e] = face_out[0, e]
-    spread_out(0, 0)
-    scatter(1, half_y)
-    spread_out(1, 0)
+    pool_both = both_cores(pool_all, jnp.concatenate([pool_in[f] for f in range(NZ)], axis=1))
+    rw[4:8] = tdot(pool_both, both_cores(gp16, gx_in[1])).reshape(4, NY, 2, NX, Q, L)
+    reduce_half(2, lambda yy, xx: rw[:, yy, c, xx])
+
+    done(w2_in, W2_).wait_recv()
+    ry[...] = tdot(
+        both_cores(w2[:, half], w2_in[...]), both_cores(gx_out[2], gx_in[2])
+    ).reshape(NZ, NY, NX, Q, L)
+    reduce_half(1, lambda yy, xx: ry[:, yy, xx])
 
     gsend[...] = gp32.reshape(NZ, Q, L)
     for other, to in on_line():
         send(gsend.at[other], grecv.at[z], GP_, to)
     grecv[z] = gsend[z]
-    scatter(2, half_w)
-    spread_out(2, 0)
-    spread_out(0, 1)
-    spread_out(1, 1)
-    spread_out(2, 1)
+    for part in range(1, len(PARTS)):
+        for n in (0, 2, 1):
+            spread_out(n, part)
 
     done(grecv.at[pl.ds(0, NZ - 1)], GP_).wait_recv()
     gp_own = jnp.concatenate([grecv[f] for f in range(NZ)], axis=1).astype(BF16)
     o_self[...] = ntdot(gp_own, wtop[...])
 
     def finish(n, part):
-        rows_at = pl.ds(part * PART, PART)
-        done(face_in.at[n, pl.ds(0, NE - 1), rows_at], FACE_ + 2 * n + part).wait_recv()
+        rows_at = rows_of(part)
+        done(face_in.at[n, pl.ds(0, NE - 1), rows_at], FACE_ + 3 * n + part).wait_recv()
         acc = face_in[n, 0, rows_at].astype(F32)
         for k in range(1, NE):
             acc = acc + face_in[n, k, rows_at].astype(F32)
-        first = part * (NZ // 2)
-        line_out[n, first:first + NZ // 2] = acc.reshape(NZ // 2, Q, L)
-        for to_z in range(first, first + NZ // 2):
+        first, end = PARTS[part]
+        line_out[n, first:end] = acc.reshape(end - first, Q, L)
+        for to_z in range(first, end):
             @pl.when(z == to_z)
             def _():
                 line_in[n, to_z] = line_out[n, to_z]
@@ -343,8 +355,8 @@
         done(line_in.at[n, pl.ds(0, NZ - 1)], LINE_ + n).wait_recv()
         return jnp.concatenate([line_in[n, f] for f in range(NZ)], axis=1)
 
-    for part in range(2):
-        for n in range(3):
+    for part in range(len(PARTS)):
+        for n in (0, 2, 1):
             finish(n, part)
     before = row_sums(0)
     rest = before - before.astype(BF16).astype(F32)
@@ -356,8 +368,9 @@
     for ref, row in (
         (qi.at[pl.ds(0, NZ - 1)], QI_), (sf_all.at[pl.ds(0, NZ - 1)], SF_),
         (t_all.at[c], TP_), (pooled.at[pl.ds(0, NZ - 1)], PO_),
-        (parts.at[pl.ds(0, NZ - 1)], PC_), (gsend.at[pl.ds(0, NZ - 1)], GP_),
+        (parts.at[pl.ds(0, NZ - 1), sent_rows], PC_), (gsend.at[pl.ds(0, NZ - 1)], GP_),
         (ps_out.at[pl.ds(0, NZ - 1)], PS_), (hot.at[0, :, away], HP_), (gx_out, GX_),
+        (w2.at[:, away], W2_), (pooled, PB_), (sf_all, SB_),
     ):
         done(ref, row).wait_send()
     for k in range(NZ):
@@ -365,11 +378,9 @@
             done(t_all.at[c, b], TZ_ + k).wait_send()
         done(t_all.at[c, pl.ds(0, NY - 1)], TY_ + k).wait_send()
     for n in range(3):
-        if n:
-            done(half_out.at[n], HALF_ + n).wait_send()
-        for part in range(2):
-            rows_at = pl.ds(part * PART, PART)
-            done(face_out.at[n, pl.ds(0, NE - 1), rows_at], FACE_ + 2 * n + part).wait_send()
+        for part in range(len(PARTS)):
+            rows_at = rows_of(part)
+            done(face_out.at[n, pl.ds(0, NE - 1), rows_at], FACE_ + 3 * n + part).wait_send()
         done(line_out.at[n, pl.ds(0, NZ - 1)], LINE_ + n).wait_send()
 
 
@@ -409,8 +420,8 @@
             V((C, G, L), F32),
             V((G, ITEMS), BF16),
             V((G, HALF), BF16),
-            V((G, L), BF16),
-            V((G, L), BF16),
+            V((3, G, L), BF16),
+            V((3, G, L), BF16),
             V((NZ, K * Q, L), BF16),
             V((NZ, K * Q, L), BF16),
             V((NZ, (C + 1) * Q, L), BF16),
@@ -420,14 +431,15 @@
             V((1024, 1024), BF16),
             V((NZ, NY, NX, Q, L), F32),
             V((NZ, NY, 2, NX, Q, L), F32),
-            V((2, NZ, NY, NX, Q, L), F32),
-            V((3, NE, G, L), BF16),
-            V((3, NE, G, L), BF16),
+            V((NZ, NY, NX, Q, L), F32),
+            V((NZ, G, L), BF16),
+            V((NZ, 2 * Q, 512), BF16),
+            V((G, HALF), BF16),
             V((3, NE, G, L), BF16),
             V((3, NE, G, L), BF16),
             V((3, NZ, Q, L), F32),
             V((3, NZ, Q, L), F32),
-            pltpu.SemaphoreType.DMA((37, 2)),
+            pltpu.SemaphoreType.DMA((40, 2)),
             pltpu.SemaphoreType.DMA((8,)),
         ],
         compiler_params=pltpu.CompilerParams(

time: 47.4 us -> 46.6 us (0.983)
  Pallas kernels: 46.6 us -> 45.8 us
    pallas_call x1, Pallas kernels: 45.1 us -> 44.4 us  [local(): pl.pallas_call(kernel, out_shape=(out, out, out), in_specs=[hbm] * 6, out...]
where the time goes in v6:
time: 46.6 us; the launch traced here: 46.5 us
  Pallas kernels  45.8 us (98%)
  between operations  0.64 us (1%)
    pallas_call x1, Pallas kernels, local(): pl.pallas_call(kernel, out_shape=(out, out, out), in_specs=[hbm] * 6, out...  44.4 us
    pallas_call x1, Pallas kernels, local(): pl.pallas_call(hand_over, out_shape=(out, out, out), in_specs=[vmem] * 3,...  1.43 us

profile of v6, /device:TPU:1, one launch (start us, length us, event | category | flops | bytes accessed | tf_op | source)
XLA Modules:
  0.0 46.5 jit_solution(10147619106110375843)
XLA Ops:
  0.6 44.4 %shard_map.85 = (f32[8,1024]{1,0:T(8,128)}, f32[8,1024]{1,0:T(8,128)}, f32[8,1024]{1,0:T(8,128)}) custom-call(bf16[32,1024]{1,0:T(8,128)(2,1)} %tab_hbm.1, bf16[8,1024]{1,0:T(8,128)(2,1)} %sf_hbm.1, s32[8,67]{1,0:T(8,128)} %bitcast.1, s32[8,67]{1,0:T(8,128)} %row_hbm.1, s32[8,50]{1,0:T(8,128)} %imp_hbm.1, bf16[2048,1024]{1,0:T(8,128)(2,1)} %w_hbm.1), custom_call_target="tpu_custom_call" | custom-call | tf_op jit(solution)/shard_map/pallas_call | solution.py:398
  45.0 1.4 %shard_map.86 = (f32[8,1024]{1,0:T(8,128)}, f32[8,1024]{1,0:T(8,128)}, f32[8,1024]{1,0:T(8,128)}) custom-call(f32[8,1024]{1,0:T(8,128)} %get-tuple-element.6.a, f32[8,1024]{1,0:T(8,128)} %get-tuple-element.7.b, f32[8,1024]{1,0:T(8,128)} %get-tuple-element.8.c), custom_call_target="tpu_custom_call" | custom-call | tf_op jit(solution)/shard_map/pallas_call | solution.py:449

commit v7 on v6

--- a/solution.py
+++ b/solution.py
@@ -37,8 +37,8 @@
     tab_hbm, sf_hbm, own_hbm, row_hbm, imp_hbm, w_hbm, o_self, o_w, o_t,
     tab, sf, own_in, row_in, imp_in,
     t_all, qi, sf_all, ps_out, ps_in, pooled, parts, gsend, grecv, hot, id_b, cand, w2, hot_in, gx_out, gx_in,
-    at_hi, at_lo, cand_hi, cand_lo,
-    wf, wtop, wbot, rx, rw, ry, pool_in, self_in, w2_in, face_out, face_in, line_out, line_in,
+    at_cand, at_hi, at_lo, cand_hi, cand_lo,
+    wf, wtop, wbot, hot_t, self_t, pool_t, rx, rw, ry, pool_in, self_in, w2_in, face_out, face_in, line_out, line_in,
     sems, wsem,
 ):
     s = lax.axis_index("shard")
@@ -72,6 +72,15 @@
             src_ref=ref, dst_ref=ref, send_sem=sems.at[row, 0], recv_sem=sems.at[row, 1],
             device_id=partner, device_id_type=MESH,
         )
+
+    bar = pltpu.get_barrier_semaphore()
+
+    def greet(to):
+        pl.semaphore_signal(bar, inc=1, device_id=to, device_id_type=MESH)
+
+    for _, to in [*on_line(), *on_face()]:
+        greet(to)
+    greet(partner)
 
     zcol = pl.ds(pl.multiple_of(z * L, L), L)
     loads = [
@@ -87,14 +96,6 @@
     for load in small + loads:
         load.start()
 
-    bar = pltpu.get_barrier_semaphore()
-
-    def greet(to):
-        pl.semaphore_signal(bar, inc=1, device_id=to, device_id_type=MESH)
-
-    for _, to in [*on_line(), *on_face()]:
-        greet(to)
-    greet(partner)
     small[3].wait()
     t_all[c, b] = tab[:, zcol]
     pl.semaphore_wait(bar, NZ - 1 + NE - 1 + 1)
@@ -158,12 +159,16 @@
         return jnp.where(spread(values, k) == lane, weight, 0.0)
 
     def outer(out, hi, lo):
-        for m in range(NZ // 2):
+        def block(m, carry):
             one = tdot(hi[2 * m], lo[2 * m])
             two = tdot(hi[2 * m + 1], lo[2 * m + 1])
+            rows_at = pl.ds(pl.multiple_of(2 * m * Q, 2 * Q), 2 * Q)
             for h in range(ITEMS // L):
                 both = jnp.concatenate([one[h * Q:(h + 1) * Q], two[h * Q:(h + 1) * Q]], axis=0)
-                out[2 * m * Q:2 * (m + 1) * Q, h * L:(h + 1) * L] = both.astype(BF16)
+                out[rows_at, h * L:(h + 1) * L] = both.astype(BF16)
+            return carry
+
+        lax.fori_loop(0, NZ // 2, block, 0)
 
     for m in range(K // 2):
         k = 2 * m
@@ -210,6 +215,8 @@
         k = K + 2 * m
         last = zero if 2 * m + 1 == C else hit(ids_hi, k + 1)
         cand_hi[:, 2 * m * Q:(2 * m + 2) * Q] = pair(hit(ids_hi, k), last)
+    for k in range(C):
+        at_cand[k] = hit(ids_lo, K + k)
     loads[0].wait()
     done(pooled.at[pl.ds(0, NZ - 1)], PO_).wait_recv()
     pool_all = jnp.concatenate([pooled[f] for f in range(NZ)], axis=1)
@@ -228,10 +235,20 @@
     parts[z, Q:Q + 1] = jnp.sum(jnp.where(row == lane, squares, 0.0), axis=0, keepdims=True)
     for _, to in on_line():
         send(parts.at[z, sent_rows], parts.at[z, sent_rows], PC_, to)
+    def both_cores(mine, theirs):
+        return jnp.concatenate([mine, theirs], axis=0)
+
     done(sf_all.at[pl.ds(0, NZ - 1)], SF_).wait_recv()
     self2 = sf_all[...].reshape(2 * G, 512)
     send(pooled, pool_in, PB_, partner)
     send(sf_all, self_in, SB_, partner)
+    done(hot_in, HP_).wait_recv()
+    hot_t[...] = both_cores(hot[0, :, half], hot_in[...]).T
+    done(pool_in, PB_).wait_recv()
+    done(self_in, SB_).wait_recv()
+    self_t[...] = both_cores(self2, self_in[...].reshape(2 * G, 512)).T
+    pool_t[...] = both_cores(
+        pool_all, jnp.concatenate([pool_in[f] for f in range(NZ)], axis=1)).T
     done(parts.at[pl.ds(0, NZ - 1), sent_rows], PC_).wait_recv()
     total, squares = parts[0, 0:Q], parts[0, Q:Q + 1]
     for f in range(1, NZ):
@@ -276,9 +293,6 @@
         face_in[n, e] = face_out[n, e]
         spread_out(n, 0)
 
-    def both_cores(mine, theirs):
-        return jnp.concatenate([mine, theirs], axis=0)
-
     def two_blocks(rows):
         blank = jnp.zeros((Q, L), F32)
         pieces = []
@@ -294,26 +308,23 @@
     send(gx_out, gx_in, GX_, partner)
     for m in range((C + 1) // 2):
         k = 2 * m
-        last = zero if k + 1 == C else hit(ids_lo, K + k + 1, coef(k + 1))
-        cand_lo[:, k * Q:(k + 2) * Q] = pair(hit(ids_lo, K + k, coef(k)), last)
+        last = zero if k + 1 == C else at_cand[k + 1] * coef(k + 1)
+        cand_lo[:, k * Q:(k + 2) * Q] = pair(at_cand[k] * coef(k), last)
     outer(w2, cand_hi, cand_lo)
     send(w2.at[:, away], w2_in, W2_, partner)
-    done(hot_in, HP_).wait_recv()
     done(gx_in, GX_).wait_recv()
 
-    rx[...] = tdot(
-        both_cores(hot[0, :, half], hot_in[...]), both_cores(gx_out[0], gx_in[0])
+    rx[...] = jnp.dot(
+        hot_t[...], both_cores(gx_out[0], gx_in[0]), preferred_element_type=F32
     ).reshape(NZ, NY, NX, Q, L)
     reduce_half(0, lambda yy, xx: rx[:, yy, xx])
 
-    done(pool_in, PB_).wait_recv()
-    done(self_in, SB_).wait_recv()
-    self_rows = both_cores(self2, self_in[...].reshape(2 * G, 512))
-    gw_self = tdot(self_rows, both_cores(two_blocks(gp16), two_blocks(gx_in[1])))
+    gw_self = jnp.dot(
+        self_t[...], both_cores(two_blocks(gp16), two_blocks(gx_in[1])), preferred_element_type=F32)
     rw[0:2] = gw_self[:, :L].reshape(2, NY, 2, NX, Q, L)
     rw[2:4] = gw_self[:, L:].reshape(2, NY, 2, NX, Q, L)
-    pool_both = both_cores(pool_all, jnp.concatenate([pool_in[f] for f in range(NZ)], axis=1))
-    rw[4:8] = tdot(pool_both, both_cores(gp16, gx_in[1])).reshape(4, NY, 2, NX, Q, L)
+    gw_pool = jnp.dot(pool_t[...], both_cores(gp16, gx_in[1]), preferred_element_type=F32)
+    rw[4:8] = gw_pool.reshape(4, NY, 2, NX, Q, L)
     reduce_half(2, lambda yy, xx: rw[:, yy, c, xx])
 
     done(w2_in, W2_).wait_recv()
@@ -422,6 +433,7 @@
             V((G, HALF), BF16),
             V((3, G, L), BF16),
             V((3, G, L), BF16),
+            V((C, G, L), F32),
             V((NZ, K * Q, L), BF16),
             V((NZ, K * Q, L), BF16),
             V((NZ, (C + 1) * Q, L), BF16),
@@ -429,6 +441,9 @@
             V((1024, L), BF16),
             V((1024, 1024), BF16),
             V((1024, 1024), BF16),
+            V((HALF, 2 * G), BF16),
+            V((512, 4 * G), BF16),
+            V((1024, 2 * G), BF16),
             V((NZ, NY, NX, Q, L), F32),
             V((NZ, NY, 2, NX, Q, L), F32),
             V((NZ, NY, NX, Q, L), F32),

time: 46.6 us -> 46.4 us (level)
  no operation moved by 1% of the time
where the time goes in v7:
time: 46.4 us; the launch traced here: 46.3 us
  Pallas kernels  45.6 us (98%)
  between operations  0.64 us (1%)
    pallas_call x1, Pallas kernels, local(): pl.pallas_call(kernel, out_shape=(out, out, out), in_specs=[hbm] * 6, out...  44.2 us
    pallas_call x1, Pallas kernels, local(): pl.pallas_call(hand_over, out_shape=(out, out, out), in_specs=[vmem] * 3,...  1.43 us

profile of v7, /device:TPU:1, one launch (start us, length us, event | category | flops | bytes accessed | tf_op | source)
XLA Modules:
  0.0 46.3 jit_solution(1668614202266408970)
XLA Ops:
  0.6 44.2 %shard_map.85 = (f32[8,1024]{1,0:T(8,128)}, f32[8,1024]{1,0:T(8,128)}, f32[8,1024]{1,0:T(8,128)}) custom-call(bf16[32,1024]{1,0:T(8,128)(2,1)} %tab_hbm.1, bf16[8,1024]{1,0:T(8,128)(2,1)} %sf_hbm.1, s32[8,67]{1,0:T(8,128)} %bitcast.1, s32[8,67]{1,0:T(8,128)} %row_hbm.1, s32[8,50]{1,0:T(8,128)} %imp_hbm.1, bf16[2048,1024]{1,0:T(8,128)(2,1)} %w_hbm.1), custom_call_target="tpu_custom_call" | custom-call | tf_op jit(solution)/shard_map/pallas_call | solution.py:409
  44.8 1.4 %shard_map.86 = (f32[8,1024]{1,0:T(8,128)}, f32[8,1024]{1,0:T(8,128)}, f32[8,1024]{1,0:T(8,128)}) custom-call(f32[8,1024]{1,0:T(8,128)} %get-tuple-element.6.a, f32[8,1024]{1,0:T(8,128)} %get-tuple-element.7.b, f32[8,1024]{1,0:T(8,128)} %get-tuple-element.8.c), custom_call_target="tpu_custom_call" | custom-call | tf_op jit(solution)/shard_map/pallas_call | solution.py:464

commit v8 on v7

--- a/solution.py
+++ b/solution.py
@@ -183,15 +183,16 @@
         for dy in range(1, NY):
             at = t_all.at[c, first + ((y + dy) & (NY - 1))]
             send(at, at, TP_, partner)
+    half = pl.ds(pl.multiple_of(c * HALF, HALF), HALF)
+    away = pl.ds(pl.multiple_of((1 - c) * HALF, HALF), HALF)
+    near = jnp.dot(hot[0, :, half], t_all[c].reshape(HALF, L), preferred_element_type=F32)
     done(t_all.at[1 - c], TP_).wait_recv()
-
-    rows = t_all[...].reshape(ITEMS, L)
-    mine = jnp.dot(hot[0], rows, preferred_element_type=F32) * inv
+    far = jnp.dot(hot[0, :, away], t_all[1 - c].reshape(HALF, L), preferred_element_type=F32)
+    mine = (near + far) * inv
     pooled[z] = mine.astype(BF16)
     for _, to in on_line():
         send(pooled.at[z], pooled.at[z], PO_, to)
-    half = pl.ds(pl.multiple_of(c * HALF, HALF), HALF)
-    away = pl.ds(pl.multiple_of((1 - c) * HALF, HALF), HALF)
+    rows = t_all[...].reshape(ITEMS, L)
     send(hot.at[0, :, away], hot_in, HP_, partner)
     for k in range(C):
         id_b[k] = spread(ids, K + k)

time: 46.4 us -> 46.6 us (level)
  no operation moved by 1% of the time
where the time goes in v8:
time: 46.6 us; the launch traced here: 46.4 us
  Pallas kernels  45.8 us (98%)
  between operations  0.64 us (1%)
    pallas_call x1, Pallas kernels, local(): pl.pallas_call(kernel, out_shape=(out, out, out), in_specs=[hbm] * 6, out...  44.4 us
    pallas_call x1, Pallas kernels, local(): pl.pallas_call(hand_over, out_shape=(out, out, out), in_specs=[vmem] * 3,...  1.43 us

profile of v8, /device:TPU:1, one launch (start us, length us, event | category | flops | bytes accessed | tf_op | source)
XLA Modules:
  0.0 46.4 jit_solution(13479065996089215698)
XLA Ops:
  0.6 44.4 %shard_map.85 = (f32[8,1024]{1,0:T(8,128)}, f32[8,1024]{1,0:T(8,128)}, f32[8,1024]{1,0:T(8,128)}) custom-call(bf16[32,1024]{1,0:T(8,128)(2,1)} %tab_hbm.1, bf16[8,1024]{1,0:T(8,128)(2,1)} %sf_hbm.1, s32[8,67]{1,0:T(8,128)} %bitcast.1, s32[8,67]{1,0:T(8,128)} %row_hbm.1, s32[8,50]{1,0:T(8,128)} %imp_hbm.1, bf16[2048,1024]{1,0:T(8,128)(2,1)} %w_hbm.1), custom_call_target="tpu_custom_call" | custom-call | tf_op jit(solution)/shard_map/pallas_call | solution.py:410
  45.0 1.4 %shard_map.86 = (f32[8,1024]{1,0:T(8,128)}, f32[8,1024]{1,0:T(8,128)}, f32[8,1024]{1,0:T(8,128)}) custom-call(f32[8,1024]{1,0:T(8,128)} %get-tuple-element.6.a, f32[8,1024]{1,0:T(8,128)} %get-tuple-element.7.b, f32[8,1024]{1,0:T(8,128)} %get-tuple-element.8.c), custom_call_target="tpu_custom_call" | custom-call | tf_op jit(solution)/shard_map/pallas_call | solution.py:465
